TPU v7x, 32 devices: a whole 2x2x4 slice. The times are simulated.
32 devices in a mesh: dp: 8 (over y, x, core), fsdp: 4 (over z).
Axes of the slice: x: 2, y: 2, z: 4, core: 2. Of those that a mesh axis runs over, the one named last changes fastest.
Arguments:
- document_tokens: bfloat16 [32, 512, 768], P(('dp', 'fsdp')), may hold values from -6 to 6
- document_lengths: int32 [32, 4], P(('dp', 'fsdp')), may hold values from 1 to 256, 488 in all within a row
- query_tokens: bfloat16 [256, 32, 768], P(('dp', 'fsdp')), may hold values from -6 to 6
- query_lengths: int32 [256], P(('dp', 'fsdp')), may hold values from 16 to 32
- weight_query: bfloat16 [589824], P(('dp', 'fsdp')), may hold values from -0.0546875 to 0.0546875
- weight_key: bfloat16 [589824], P(('dp', 'fsdp')), may hold values from -0.21875 to 0.21875
- weight_value: bfloat16 [589824], P(('dp', 'fsdp')), may hold values from -0.21875 to 0.21875
- weight_out: bfloat16 [589824], P(('dp', 'fsdp')), may hold values from -0.625 to 0.625
- weight_gate: bfloat16 [2359296], P(('dp', 'fsdp')), may hold values from -0.21875 to 0.21875
- weight_up: bfloat16 [2359296], P(('dp', 'fsdp')), may hold values from -0.21875 to 0.21875
- weight_down: bfloat16 [2359296], P(('dp', 'fsdp')), may hold values from -0.15625 to 0.15625
- weight_proj: bfloat16 [98304], P(('dp', 'fsdp')), may hold values from -0.21875 to 0.21875
- norm_gains: bfloat16 [2304], P('fsdp'), may hold values from 0.099609375 to 1.8984375
- rel_table: bfloat16 [384], P('fsdp'), may hold values from -4 to 4
- document_cotangent: bfloat16 [32, 512, 128], P(('dp', 'fsdp')), may hold values from -6 to 6
- query_cotangent: bfloat16 [256, 32, 128], P(('dp', 'fsdp')), may hold values from -6 to 6
Outputs:
- document_output: bfloat16 [32, 512, 128], P(('dp', 'fsdp'))
- query_output: bfloat16 [256, 32, 128], P(('dp', 'fsdp'))
- document_grad: bfloat16 [32, 512, 768], P(('dp', 'fsdp'))
- query_grad: bfloat16 [256, 32, 768], P(('dp', 'fsdp'))
- grad_query: float32 [589824], P(('dp', 'fsdp'))
- grad_key: float32 [589824], P(('dp', 'fsdp'))
- grad_value: float32 [589824], P(('dp', 'fsdp'))
- grad_out: float32 [589824], P(('dp', 'fsdp'))
- grad_gate: float32 [2359296], P(('dp', 'fsdp'))
- grad_up: float32 [2359296], P(('dp', 'fsdp'))
- grad_down: float32 [2359296], P(('dp', 'fsdp'))
- grad_proj: float32 [98304], P(('dp', 'fsdp'))
- grad_gains: float32 [2304], P('fsdp')
- grad_table: float32 [384], P('fsdp')
Inputs may be any that keep to these rules, and one draw needn't show every extreme that they name: `document_lengths`: in every row the 4 lengths sum to 488, and the longest is 256; positions from 488 on are padding. `query_lengths`: positions from a query's length on are padding.
All inputs are finite; a program needn't handle non-finite values.
Results may differ from a plain program's by a relative error of at most 0.014.
The roundings to bfloat16 on the way count: a program that leaves them out, or rounds other values in their place, can miss the bound.
Values may be sent and summed in bfloat16 or wider, within the bound.
A program may use at most 256 MiB of HBM per device.

v0:
```python
import jax
import jax.numpy as jnp
from jax import lax
from jax.sharding import PartitionSpec as P

D = 768
HEADS = 12
HEAD_DIM = 64
FF = 3072
BUCKETS = 32
PROJ = 128
DOC_LEN = 512
QRY_LEN = 32


EPSILON = 1e-06
NEGATIVE = -1e30


def rms_norm(values, gain_row):
    inverse = lax.rsqrt(jnp.mean(values * values, axis=-1, keepdims=True) + EPSILON)
    return values * inverse * gain_row


def gated_unit(gate_in, upper_in):
    return jax.nn.gelu(gate_in, approximate=True) * upper_in


def bucket_ids(length):
    positions = jnp.arange(length, dtype=jnp.int32)
    relative = positions[None, :] - positions[:, None]
    distance = jnp.abs(relative)
    distant = 8 + sum(
        ((distance * distance >= 64 * 2**power).astype(jnp.int32) for power in range(1, 8))
    )
    nearby = jnp.where(distance < 8, distance, distant)
    return nearby + 16 * (relative > 0).astype(jnp.int32)


def bucket_onehot(length):
    flat_ids = bucket_ids(length).reshape(1, length * length)
    labels = jnp.arange(BUCKETS, dtype=jnp.int32).reshape(BUCKETS, 1)
    return (flat_ids == labels).astype(jnp.bfloat16)


def segment_ids(lengths, length):
    boundary = jnp.cumsum(lengths, axis=-1)
    positions = jnp.arange(length, dtype=jnp.int32)
    return jnp.sum((positions[None, :, None] >= boundary[:, None, :]).astype(jnp.int32), axis=-1)


def outer_sum(left_rows, right_rows):
    return lax.dot_general(
        left_rows, right_rows, (((0,), (0,)), ((), ())), preferred_element_type=jnp.float32
    )


def times_transposed(left_rows, matrix):
    return lax.dot_general(
        left_rows, matrix, (((1,), (1,)), ((), ())), preferred_element_type=jnp.float32
    )


def flat_piece(left_rows, right_rows, start, count):
    width = right_rows.shape[1]
    needed = count // width + 2
    padded = jnp.pad(left_rows, ((0, 0), (0, needed)))
    first_row = start // width
    columns = lax.dynamic_slice_in_dim(padded, first_row, needed, 1)
    block = outer_sum(columns, right_rows).reshape(-1)
    return lax.dynamic_slice_in_dim(block, start, count)


def grad_terms(pairs, devices):
    shares = [pair[0].shape[1] * pair[1].shape[1] // devices for pair in pairs]
    total_share = sum(shares)

    def term(start, count):
        blocks = count // total_share
        first_block = start // total_share
        pieces = [
            flat_piece(pair[0], pair[1], first_block * share, blocks * share).reshape(blocks, share)
            for pair, share in zip(pairs, shares)
        ]
        return jnp.concatenate(pieces, axis=1).reshape(-1)

    return (term, total_share, shares)


def split_shares(mine, shares):
    results = []
    offset = 0
    for share in shares:
        results.append(mine[offset : offset + share])
        offset = offset + share
    return results


def bias_rows(table_mat, onehot, length):
    rel_bias = lax.dot_general(
        table_mat, onehot, (((0,), (0,)), ((), ())), preferred_element_type=jnp.float32
    )
    return rel_bias.reshape(1, HEADS, length, length)


def masked_scores(queries, key_rows, rel_bias, allowed):
    scores = (
        jnp.einsum("bqhd,bkhd->bhqk", queries, key_rows, preferred_element_type=jnp.float32)
        + rel_bias
    )
    return jnp.where(allowed, scores, NEGATIVE)


def attend(queries, key_rows, values, rel_bias, allowed):
    scores = masked_scores(queries, key_rows, rel_bias, allowed)
    largest = jnp.max(scores, axis=-1, keepdims=True)
    summed = jnp.sum(jnp.exp(scores - largest), axis=-1, keepdims=True)
    log_total = largest + jnp.log(summed)
    attention = jnp.exp(scores - log_total).astype(jnp.bfloat16)
    context = jnp.einsum("bhqk,bkhd->bqhd", attention, values, preferred_element_type=jnp.float32)
    return (context.astype(jnp.bfloat16), log_total)


def attend_back(queries, key_rows, values, rel_bias, allowed, log_total, grad_context):
    scores = masked_scores(queries, key_rows, rel_bias, allowed)
    attention = jnp.exp(scores - log_total)
    grad_attention = jnp.einsum(
        "bqhd,bkhd->bhqk", grad_context, values, preferred_element_type=jnp.float32
    )
    grad_values = jnp.einsum(
        "bhqk,bqhd->bkhd",
        attention.astype(jnp.bfloat16),
        grad_context,
        preferred_element_type=jnp.float32,
    )
    weighted = jnp.sum(attention * grad_attention, axis=-1, keepdims=True)
    grad_scores = (attention * (grad_attention - weighted)).astype(jnp.bfloat16)
    grad_queries = jnp.einsum(
        "bhqk,bkhd->bqhd", grad_scores, key_rows, preferred_element_type=jnp.float32
    )
    grad_keys = jnp.einsum(
        "bhqk,bqhd->bkhd", grad_scores, queries, preferred_element_type=jnp.float32
    )
    return (
        grad_queries.astype(jnp.bfloat16),
        grad_keys.astype(jnp.bfloat16),
        grad_values.astype(jnp.bfloat16),
        grad_scores,
    )


def bias_grads(grad_scores, onehot):
    members = grad_scores.shape[0]
    flattened = grad_scores.reshape(members * HEADS, -1)
    summed = lax.dot_general(
        flattened, onehot, (((1,), (1,)), ((), ())), preferred_element_type=jnp.float32
    )
    return jnp.sum(summed.reshape(members, HEADS, BUCKETS), axis=0)


def local(
    document_tokens,
    document_lengths,
    query_tokens,
    query_lengths,
    weight_query,
    weight_key,
    weight_value,
    weight_out,
    weight_gate,
    weight_up,
    weight_down,
    weight_proj,
    norm_gains,
    rel_table,
    document_cotangent,
    query_cotangent,
):
    layouts = ((D, D), (D, D), (D, D), (D, D), (D, FF), (D, FF), (FF, D), (D, PROJ))
    devices = lax.axis_size("dp") * lax.axis_size("fsdp")
    gathered = (
        lax.all_gather(weight_query, ("dp", "fsdp"), axis=0, tiled=True),
        lax.all_gather(weight_key, ("dp", "fsdp"), axis=0, tiled=True),
        lax.all_gather(weight_value, ("dp", "fsdp"), axis=0, tiled=True),
        lax.all_gather(weight_out, ("dp", "fsdp"), axis=0, tiled=True),
        lax.all_gather(weight_gate, ("dp", "fsdp"), axis=0, tiled=True),
        lax.all_gather(weight_up, ("dp", "fsdp"), axis=0, tiled=True),
        lax.all_gather(weight_down, ("dp", "fsdp"), axis=0, tiled=True),
        lax.all_gather(weight_proj, ("dp", "fsdp"), axis=0, tiled=True),
    )
    matrices = [flat_rows.reshape(layout) for flat_rows, layout in zip(gathered, layouts)]
    gains_all, table_all = (
        lax.all_gather(norm_gains, "fsdp", axis=0, tiled=True),
        lax.all_gather(rel_table, "fsdp", axis=0, tiled=True),
    )
    gain_rows = gains_all.astype(jnp.float32).reshape(3, D)
    table_mat = table_all.reshape(BUCKETS, HEADS)
    documents = document_tokens.shape[0]
    queries_here = query_tokens.shape[0]
    doc_rows = documents * DOC_LEN
    doc_segments = segment_ids(document_lengths, DOC_LEN)
    query_segments = segment_ids(query_lengths.reshape(queries_here, 1), QRY_LEN)
    doc_allowed = doc_segments[:, None, :, None] == doc_segments[:, None, None, :]
    query_allowed = query_segments[:, None, :, None] == query_segments[:, None, None, :]
    doc_onehot = bucket_onehot(DOC_LEN)
    query_onehot = bucket_onehot(QRY_LEN)
    doc_bias = bias_rows(table_mat, doc_onehot, DOC_LEN)
    query_bias = bias_rows(table_mat, query_onehot, QRY_LEN)
    settings = [(doc_bias, doc_allowed, doc_onehot)]
    settings.append((query_bias, query_allowed, query_onehot))

    def split_blocks(matrix):
        blocks_out = [matrix[0:DOC_LEN].reshape(1, DOC_LEN, HEADS, HEAD_DIM)]
        blocks_out.append(matrix[doc_rows:].reshape(queries_here, QRY_LEN, HEADS, HEAD_DIM))
        return blocks_out

    query_mat, key_mat, value_mat, out_mat, gate_mat, up_mat, down_mat, proj_mat = matrices
    inputs = jnp.concatenate(
        [document_tokens.reshape(doc_rows, D), query_tokens.reshape(-1, D)], axis=0
    )
    residual_in = inputs.astype(jnp.float32)
    normed_one, norm_one_back = jax.vjp(rms_norm, residual_in, gain_rows[0])
    normed_one = normed_one.astype(jnp.bfloat16)
    queries = jnp.dot(normed_one, query_mat, preferred_element_type=jnp.float32).astype(
        jnp.bfloat16
    )
    key_rows = jnp.dot(normed_one, key_mat, preferred_element_type=jnp.float32).astype(jnp.bfloat16)
    values = jnp.dot(normed_one, value_mat, preferred_element_type=jnp.float32).astype(jnp.bfloat16)
    query_blocks = split_blocks(queries)
    key_blocks = split_blocks(key_rows)
    value_blocks = split_blocks(values)
    contexts = []
    log_totals = []
    for query_block, key_block, value_block, setting in zip(
        query_blocks, key_blocks, value_blocks, settings
    ):
        context_block, log_total = attend(
            query_block, key_block, value_block, setting[0], setting[1]
        )
        contexts.append(context_block.reshape(-1, D))
        log_totals.append(log_total)
    context = jnp.concatenate(contexts, axis=0)
    hidden = residual_in + jnp.dot(context, out_mat, preferred_element_type=jnp.float32)
    normed_two, norm_two_back = jax.vjp(rms_norm, hidden, gain_rows[1])
    normed_two = normed_two.astype(jnp.bfloat16)
    gate = jnp.dot(normed_two, gate_mat, preferred_element_type=jnp.float32)
    upper = jnp.dot(normed_two, up_mat, preferred_element_type=jnp.float32)
    inner, gated_back = jax.vjp(gated_unit, gate, upper)
    inner = inner.astype(jnp.bfloat16)
    final = hidden + jnp.dot(inner, down_mat, preferred_element_type=jnp.float32)
    normed_three, norm_three_back = jax.vjp(rms_norm, final, gain_rows[2])
    normed_three = normed_three.astype(jnp.bfloat16)
    output = jnp.dot(normed_three, proj_mat, preferred_element_type=jnp.float32).astype(
        jnp.bfloat16
    )
    again = (
        lax.all_gather(weight_query, ("dp", "fsdp"), axis=0, tiled=True),
        lax.all_gather(weight_key, ("dp", "fsdp"), axis=0, tiled=True),
        lax.all_gather(weight_value, ("dp", "fsdp"), axis=0, tiled=True),
        lax.all_gather(weight_out, ("dp", "fsdp"), axis=0, tiled=True),
        lax.all_gather(weight_gate, ("dp", "fsdp"), axis=0, tiled=True),
        lax.all_gather(weight_up, ("dp", "fsdp"), axis=0, tiled=True),
        lax.all_gather(weight_down, ("dp", "fsdp"), axis=0, tiled=True),
        lax.all_gather(weight_proj, ("dp", "fsdp"), axis=0, tiled=True),
    )
    back_mats = [flat_rows.reshape(layout) for flat_rows, layout in zip(again, layouts)]
    back_query, back_key, back_value, back_out, back_gate, back_up, back_down, back_proj = back_mats
    cotangent = jnp.concatenate(
        [document_cotangent.reshape(doc_rows, PROJ), query_cotangent.reshape(-1, PROJ)], axis=0
    )
    grad_final, grad_gain_three = norm_three_back(times_transposed(cotangent, back_proj))
    grad_ffn = grad_final.astype(jnp.bfloat16)
    grad_gate_f, grad_upper_f = gated_back(times_transposed(grad_ffn, back_down))
    grad_gate_b = grad_gate_f.astype(jnp.bfloat16)
    grad_upper_b = grad_upper_f.astype(jnp.bfloat16)
    grad_normed_two = times_transposed(grad_gate_b, back_gate) + times_transposed(
        grad_upper_b, back_up
    )
    grad_hidden_part, grad_gain_two = norm_two_back(grad_normed_two)
    grad_hidden = grad_final + grad_hidden_part
    ffn_pairs = [
        (normed_two, grad_gate_b),
        (normed_two, grad_upper_b),
        (inner, grad_ffn),
        (normed_three, cotangent),
    ]
    grad_branch = grad_hidden.astype(jnp.bfloat16)
    grad_context = times_transposed(grad_branch, back_out).astype(jnp.bfloat16)
    table_grad = jnp.zeros((HEADS, BUCKETS), jnp.float32)
    grad_query_parts = []
    grad_key_parts = []
    grad_value_parts = []
    for query_block, key_block, value_block, setting, log_total, grad_block in zip(
        query_blocks, key_blocks, value_blocks, settings, log_totals, split_blocks(grad_context)
    ):
        grad_q_block, grad_k_block, grad_v_block, grad_scores = attend_back(
            query_block, key_block, value_block, setting[0], setting[1], log_total, grad_block
        )
        table_grad = table_grad + bias_grads(grad_scores, setting[2])
        grad_query_parts.append(grad_q_block.reshape(-1, D))
        grad_key_parts.append(grad_k_block.reshape(-1, D))
        grad_value_parts.append(grad_v_block.reshape(-1, D))
    grad_queries = jnp.concatenate(grad_query_parts, axis=0)
    grad_keys = jnp.concatenate(grad_key_parts, axis=0)
    grad_values = jnp.concatenate(grad_value_parts, axis=0)
    grad_normed_one = (
        times_transposed(grad_queries, back_query)
        + times_transposed(grad_keys, back_key)
        + times_transposed(grad_values, back_value)
    )
    grad_input_part, grad_gain_one = norm_one_back(grad_normed_one)
    grad_inputs = (grad_hidden + grad_input_part).astype(jnp.bfloat16)
    attn_pairs = [
        (normed_one, grad_queries),
        (normed_one, grad_keys),
        (normed_one, grad_values),
        (context, grad_branch),
    ]
    all_term, all_total, all_shares = grad_terms(attn_pairs + ffn_pairs, devices)
    shares = tuple(
        split_shares(
            lax.psum_scatter(
                all_term(jnp.int32(0), lax.axis_size(("dp", "fsdp")) * all_total),
                ("dp", "fsdp"),
                scatter_dimension=0,
                tiled=True,
            ),
            all_shares,
        )
    )
    gain_grads = jnp.concatenate([grad_gain_one, grad_gain_two, grad_gain_three], axis=0)
    table_flat = jnp.transpose(table_grad).reshape(-1)
    gain_whole, table_whole = lax.psum((gain_grads, table_flat), ("dp", "fsdp"))
    fsdp_index = lax.axis_index("fsdp")
    fsdp_count = lax.axis_size("fsdp")
    gain_share = 3 * D // fsdp_count
    table_share = BUCKETS * HEADS // fsdp_count
    own_gains = lax.dynamic_slice_in_dim(gain_whole, fsdp_index * gain_share, gain_share)
    own_table = lax.dynamic_slice_in_dim(table_whole, fsdp_index * table_share, table_share)
    return (
        output[:doc_rows].reshape(documents, DOC_LEN, PROJ),
        output[doc_rows:].reshape(queries_here, QRY_LEN, PROJ),
        grad_inputs[:doc_rows].reshape(documents, DOC_LEN, D),
        grad_inputs[doc_rows:].reshape(queries_here, QRY_LEN, D),
        shares[0],
        shares[1],
        shares[2],
        shares[3],
        shares[4],
        shares[5],
        shares[6],
        shares[7],
        own_gains,
        own_table,
    )


def solution(mesh):
    placed = (
        P(("dp", "fsdp"), None, None),
        P(("dp", "fsdp"), None),
        P(("dp", "fsdp"), None, None),
        P(("dp", "fsdp")),
        P(("dp", "fsdp")),
        P(("dp", "fsdp")),
        P(("dp", "fsdp")),
        P(("dp", "fsdp")),
        P(("dp", "fsdp")),
        P(("dp", "fsdp")),
        P(("dp", "fsdp")),
        P(("dp", "fsdp")),
        P("fsdp"),
        P("fsdp"),
        P(("dp", "fsdp"), None, None),
        P(("dp", "fsdp"), None, None),
    )
    return jax.shard_map(
        local,
        mesh=mesh,
        in_specs=placed,
        out_specs=(
            P(("dp", "fsdp"), None, None),
            P(("dp", "fsdp"), None, None),
            P(("dp", "fsdp"), None, None),
            P(("dp", "fsdp"), None, None),
            P(("dp", "fsdp")),
            P(("dp", "fsdp")),
            P(("dp", "fsdp")),
            P(("dp", "fsdp")),
            P(("dp", "fsdp")),
            P(("dp", "fsdp")),
            P(("dp", "fsdp")),
            P(("dp", "fsdp")),
            P("fsdp"),
            P("fsdp"),
        ),
        check_vma=False,
    )
```

profile of v0, /device:TPU:0, one launch (start us, length us, event | category | flops | bytes accessed | tf_op | source)
XLA Modules:
  0.0 1240.6 jit_solution(8645219421527196835)
XLA Ops:
  19.4 13.9 %all-reduce.9 = (bf16[2304]{0:T(1024)(128)(2,1)S(1)}, bf16[384]{0:T(512)(128)(2,1)S(1)}) all-reduce(bf16[2304]{0:T(1024)(128)(2,1)S(1)} %dynamic-update-slice, bf16[384]{0:T(512)(128)(2,1)S(1)} %dynamic-update-slice.1), channel_id=1, replica_groups=mesh['dp'=8,'fsdp'=4] {'fsdp'}, use_global_device_ids=true, to_apply=%add.5 | all-reduce | flops 2688 | bytes 10752
  35.6 6.0 fusion.1
  41.6 19.1 %copy.214 = f32[2,8,512,512]{3,2,1,0:T(8,128)} copy(f32[2,8,512,512]{3,1,2,0:T(8,128)S(1)} %bitcast.155) | data formatting | bytes 33554432
  60.7 10.7 slice.144
  71.5 12.7 %copy.143 = f32[12,512,512]{1,2,0:T(8,128)} copy(f32[12,512,512]{2,1,0:T(8,128)} %slice.144) | data formatting | bytes 25165824 | tf_op jit(solution)/shard_map/reshape | solution.py:103
  86.0 70.2 %all_gather.47 = bf16[98304]{0:T(1024)(128)(2,1)} all-gather(bf16[3072]{0:T(1024)(128)(2,1)S(1)} %copy-done.73), channel_id=1, replica_groups=mesh['dp'=8,'fsdp'=4] {'dp','fsdp'}, dimensions={0}, use_global_device_ids=true | all-gather | bytes 202752 | tf_op jit(solution)/shard_map/all_gather | solution.py:189
  158.6 3.1 reshape.650
  164.7 2.6 reshape.652
  170.4 9.1 all-gather.8.cloned.1.call-done
  179.5 3.4 reshape.648
  182.9 2.5 convolution_convert_fusion.3
  201.9 2.7 copy.195
  204.6 3.2 reshape.732
  207.8 27.5 %all-gather.14.cloned.1.call-done = bf16[589824]{0:T(1024)(128)(2,1)} async-done(((bf16[18432]{0:T(1024)(128)(2,1)}), bf16[589824]{0:T(1024)(128)(2,1)}) %all-gather.14.cloned.1.call-update) | async-done | bytes 1179664 | tf_op jit(solution)/shard_map/all_gather | solution.py:185
  235.2 3.3 reshape.661
  238.6 6.2 fusion.106
  246.7 2.7 copy-done
  249.4 2.1 fusion.25
  254.5 46.0 %all-gather.16.cloned.1.call-done = bf16[2359296]{0:T(1024)(128)(2,1)} async-done(((bf16[73728]{0:T(1024)(128)(2,1)}), bf16[2359296]{0:T(1024)(128)(2,1)}) %all-gather.16.cloned.1.call-update) | async-done | bytes 4718608 | tf_op jit(solution)/shard_map/all_gather | solution.py:186
  300.4 8.2 reshape.662
  308.7 56.8 %all-gather.18.cloned.1.call-done = bf16[2359296]{0:T(1024)(128)(2,1)} async-done(((bf16[73728]{0:T(1024)(128)(2,1)}), bf16[2359296]{0:T(1024)(128)(2,1)}) %all-gather.18.cloned.1.call-update) | async-done | bytes 4718608 | tf_op jit(solution)/shard_map/all_gather | solution.py:187
  365.5 8.2 reshape.663
  373.7 5.9 fusion.107
  379.7 3.6 copy-done.15
  383.3 9.5 multiply_convert_fusion.2
  392.8 37.9 %all-gather.20.cloned.1.call-done = bf16[2359296]{0:T(1024)(128)(2,1)} async-done(((bf16[73728]{0:T(1024)(128)(2,1)}), bf16[2359296]{0:T(1024)(128)(2,1)}) %all-gather.20.cloned.1.call-update) | async-done | bytes 4718608 | tf_op jit(solution)/shard_map/all_gather | solution.py:188
  430.7 9.2 reshape.664
  439.9 8.7 multiply_reduce_fusion.5
  450.9 18.3 %multiply_convert_fusion.1 = (bf16[768,3072]{1,0:T(8,128)(2,1)}, bf16[768,3072]{1,0:T(8,128)(2,1)}) fusion(f32[768,3072]{1,0:T(8,128)} %copy-done.15, f32[768,3072]{1,0:T(8,128)} %get-tuple-element.101, bf16[3072,768]{1,0:T(8,128)(2,1)} %reshape.664, f32[768,768]{0,1:T(8,128)S(1)} %get-tuple-element.89), kind=kOutput, calls=%fused_computation.20 | convolution fusion | flops 3681091584 | bytes 35389440 | tf_op jit(solution)/shard_map/dot_general | solution.py:59
  469.2 6.4 fusion.108
  475.7 7.0 multiply_reduce_fusion.2
  487.1 6.0 multiply_reduce_fusion
  493.1 7.1 multiply_convert_fusion
  500.2 2.9 convolution_convert_fusion.6
  505.2 2.9 reshape.739
  508.1 2.8 copy.160
  516.3 7.8 fusion.28
  526.2 2.5 fusion.52
  528.8 6.3 fusion.109
  535.1 6.3 fusion.110
  541.4 6.7 fusion.55
  558.7 3.9 fusion.47
  564.4 4.3 fusion.48
  568.7 2.9 reshape.681
  571.5 4.1 fusion.50
  575.7 3.0 reshape.680
  578.7 3.3 constant_dynamic-update-slice_fusion.7
  582.0 3.0 reshape.683
  584.9 8.1 reshape.684
  593.0 8.2 reshape.685
  601.2 8.5 reshape.686
  609.7 2.2 fusion.67
  613.0 3.4 constant_dynamic-update-slice_fusion.6
  620.6 9.2 constant_dynamic-update-slice_fusion.3
  629.8 4.2 constant_dynamic-update-slice_fusion.2
  634.0 4.2 constant_dynamic-update-slice_fusion.1
  639.0 32.8 %copy.215 = f32[4,2328,8,128]{3,1,2,0:T(8,128)} copy(f32[4,2328,8,128]{3,2,1,0:T(8,128)} %bitcast.157) | data formatting | bytes 76283904
  671.8 8.8 copy.179
  680.9 7.0 pad.40
  688.0 11.6 copy.216
  700.7 8.3 fusion.36
  718.5 41.9 %all-reduce.8 = (f32[2304]{0:T(1024)S(1)}, f32[384]{0:T(512)S(1)}) all-reduce(f32[2304]{0:T(1024)S(1)} %pad_maximum_fusion.16, f32[384]{0:T(512)S(1)} %reshape.690), channel_id=1, replica_groups=mesh['dp'=8,'fsdp'=4] {'dp','fsdp'}, use_global_device_ids=true, to_apply=%region_18.19 | all-reduce | flops 2688 | bytes 21504 | tf_op jit(solution)/shard_map/psum | solution.py:333
  762.4 465.7 %all-reduce.12.cloned.1.call-done = f32[9535488]{0:T(1024)} async-done(((f32[9535488]{0:T(1024)}), f32[9535488]{0:T(1024)}) %all-reduce.12.cloned.1.call-update) | async-done | bytes 38141968
  1229.4 2.3 fusion.102
  (323 shorter events, 95.0 us)
Async XLA Ops:
  7.2 151.5 %all-gather.10.cloned.1.call-start = ((), (), s32[]{:S(2)}) async-start(), calls=%async_computation.1 | async-start | bytes 1216512 | tf_op jit(solution)/shard_map/all_gather | solution.py:182
  7.9 156.8 %all-gather.12.cloned.1.call-start = ((), (), s32[]{:S(2)}) async-start(), calls=%async_computation.2 | async-start | bytes 1216512 | tf_op jit(solution)/shard_map/all_gather | solution.py:183
  8.7 170.9 %all-gather.8.cloned.1.call-start = ((), (), s32[]{:S(2)}) async-start(), calls=%async_computation | async-start | bytes 1216512 | tf_op jit(solution)/shard_map/all_gather | solution.py:184
  9.4 225.8 %all-gather.14.cloned.1.call-start = ((), (), s32[]{:S(2)}) async-start(), calls=%async_computation.3 | async-start | bytes 1216512 | tf_op jit(solution)/shard_map/all_gather | solution.py:185
  10.0 290.5 %all-gather.16.cloned.1.call-start = ((), (), s32[]{:S(2)}) async-start(), calls=%async_computation.4 | async-start | bytes 4866048 | tf_op jit(solution)/shard_map/all_gather | solution.py:186
  10.6 354.9 %all-gather.18.cloned.1.call-start = ((), (), s32[]{:S(2)}) async-start(), calls=%async_computation.5 | async-start | bytes 4866048 | tf_op jit(solution)/shard_map/all_gather | solution.py:187
  11.1 419.6 %all-gather.20.cloned.1.call-start = ((), (), s32[]{:S(2)}) async-start(), calls=%async_computation.6 | async-start | bytes 4866048 | tf_op jit(solution)/shard_map/all_gather | solution.py:188
  11.9 1216.2 %all-reduce.12.cloned.1.call-start = ((), (), s32[]{:S(2)}) async-start(), calls=%async_computation.7 | async-start | bytes 76283904
  13.0 3.9 copy-start.79
  13.0 5.8 copy-start.75
  13.1 6.1 copy-start.77
  15.4 167.4 %copy-start.24 = (bf16[1,512,768]{1,2,0:T(8,128)(2,1)}, bf16[1,512,768]{1,2,0:T(8,128)(2,1)S(1)}, u32[]{:S(2)}) copy-start(bf16[1,512,768]{1,2,0:T(8,128)(2,1)S(1)} %copy.141) | copy-start | bytes 2359300
  16.9 234.5 %copy-start.35 = (bf16[256,768]{0,1:T(8,128)(2,1)}, bf16[256,768]{0,1:T(8,128)(2,1)S(1)}, u32[]{:S(2)}) copy-start(bf16[256,768]{0,1:T(8,128)(2,1)S(1)} %copy.142) | copy-start | bytes 1179652
  35.6 6.0 copy-start.33
  71.5 14.1 %copy-start.78 = (s32[1,4]{1,0:T(1,128)S(1)}, s32[1,4]{1,0:T(1,128)}, u32[]{:S(2)}) copy-start(s32[1,4]{1,0:T(1,128)} %param.17) | copy-start | bytes 52
  71.5 14.5 %copy-start.73 = (bf16[3072]{0:T(1024)(128)(2,1)S(1)}, bf16[3072]{0:T(1024)(128)(2,1)}, u32[]{:S(2)}) copy-start(bf16[3072]{0:T(1024)(128)(2,1)} %param.27) | copy-start | bytes 18436
  71.5 84.8 %copy-start.76 = (s32[8]{0:T(128)S(1)}, s32[8]{0:T(128)}, u32[]{:S(2)}) copy-start(s32[8]{0:T(128)} %param.19) | copy-start | bytes 100
  84.4 74.2 %copy-start.71 = (s32[1024]{0:T(1024)}, s32[1024]{0:T(1024)S(1)}, u32[]{:S(2)}) copy-start(s32[1024]{0:T(1024)S(1)} %fusion.81) | copy-start | bytes 12292
  86.0 75.7 %copy-start.64 = (f32[768]{0:T(1024)}, f32[768]{0:T(1024)S(1)}, u32[]{:S(2)}) copy-start(f32[768]{0:T(1024)S(1)} %fusion.19) | copy-start | bytes 9220
  156.4 26.5 %copy-start.66 = (f32[768]{0:T(1024)}, f32[768]{0:T(1024)S(1)}, u32[]{:S(2)}) copy-start(f32[768]{0:T(1024)S(1)} %fusion.83) | copy-start | bytes 9220
  157.7 4.0 copy-start.68
  185.5 61.2 %copy-start.16 = (bf16[512,768]{0,1:T(8,128)(2,1)}, bf16[512,768]{0,1:T(8,128)(2,1)S(1)}, u32[]{:S(2)}) copy-start(bf16[512,768]{0,1:T(8,128)(2,1)S(1)} %slice.130) | copy-start | bytes 2359300
  244.8 4.6 copy-start
  246.7 4.8 copy-start.54
  254.5 125.2 %copy-start.31 = (bf16[768,768]{0,1:T(8,128)(2,1)}, bf16[768,768]{0,1:T(8,128)(2,1)S(1)}, u32[]{:S(2)}) copy-start(bf16[768,768]{0,1:T(8,128)(2,1)S(1)} %multiply_convert_fusion.4) | copy-start | bytes 3538948
  373.7 9.6 copy-start.30
  439.9 8.8 copy-start.41
  439.9 8.8 copy-start.59
  439.9 8.8 copy-start.63
  450.1 19.1 %slice-start.9 = ((s8[4718592]{0:T(1024)(128)(4,1)}), s8[4194304]{0:T(1024)(128)(4,1)S(1)}, s32[]{:S(2)}) async-start(s8[4718592]{0:T(1024)(128)(4,1)} %bitcast.163), calls=%async_computation.17 | async-start | bytes 8388608
  450.9 18.3 %copy-start.11 = (f32[768,768]{0,1:T(8,128)}, f32[768,768]{0,1:T(8,128)S(1)}, u32[]{:S(2)}) copy-start(f32[768,768]{0,1:T(8,128)S(1)} %get-tuple-element.89) | copy-start | bytes 7077892
  450.9 158.9 %copy-start.7 = (bf16[768,768]{0,1:T(8,128)(2,1)}, bf16[768,768]{0,1:T(8,128)(2,1)S(1)}, u32[]{:S(2)}) copy-start(bf16[768,768]{0,1:T(8,128)(2,1)S(1)} %get-tuple-element.90) | copy-start | bytes 3538948
  450.9 18.3 %slice-start.10 = ((s8[4718592]{0:T(1024)(128)(4,1)}), s8[524288]{0:T(1024)(128)(4,1)S(1)}, s32[]{:S(2)}) async-start(s8[4718592]{0:T(1024)(128)(4,1)} %bitcast.163), calls=%async_computation.18 | async-start | bytes 1048576
  469.2 6.4 copy-start.10
  469.2 6.4 copy-start.80
  475.7 7.1 copy-start.12
  475.7 10.6 slice-start
  475.7 10.6 slice-start.1
  485.4 7.6 copy-start.18
  493.1 7.1 copy-start.20
  505.2 5.7 copy-start.22
  515.0 13.8 %slice-start.13 = ((s8[4718592]{0:T(1024)(128)(4,1)}), s8[4194304]{0:T(1024)(128)(4,1)S(1)}, s32[]{:S(2)}) async-start(s8[4718592]{0:T(1024)(128)(4,1)} %bitcast.205), calls=%async_computation.21 | async-start | bytes 8388608
  516.3 7.8 copy-start.23
  516.3 9.1 copy-start.46
  516.3 12.4 %slice-start.14 = ((s8[4718592]{0:T(1024)(128)(4,1)}), s8[524288]{0:T(1024)(128)(4,1)S(1)}, s32[]{:S(2)}) async-start(s8[4718592]{0:T(1024)(128)(4,1)} %bitcast.205), calls=%async_computation.22 | async-start | bytes 1048576
  526.2 8.9 slice-start.11
  528.8 6.4 slice-start.12
  528.8 12.6 %slice-start.15 = ((s8[4718592]{0:T(1024)(128)(4,1)}), s8[524288]{0:T(1024)(128)(4,1)S(1)}, s32[]{:S(2)}) async-start(s8[4718592]{0:T(1024)(128)(4,1)} %bitcast.207), calls=%async_computation.23 | async-start | bytes 1048576
  535.1 6.3 copy-start.13
  535.1 6.3 slice-start.16
  548.1 3.9 copy-start.39
  554.8 3.8 copy-start.69
  613.0 16.8 %slice-start.6 = ((s8[9437184]{0:T(1024)(128)(4,1)}), s8[4194304]{0:T(1024)(128)(4,1)S(1)}, s32[]{:S(2)}) async-start(s8[9437184]{0:T(1024)(128)(4,1)} %bitcast.160), calls=%async_computation.14 | async-start | bytes 8388608
  618.9 10.8 slice-start.7
  620.6 9.2 slice-start.8
  620.6 13.4 %slice-start.3 = ((s8[9437184]{0:T(1024)(128)(4,1)}), s8[4194304]{0:T(1024)(128)(4,1)S(1)}, s32[]{:S(2)}) async-start(s8[9437184]{0:T(1024)(128)(4,1)} %bitcast.158), calls=%async_computation.11 | async-start | bytes 8388608
  620.6 13.4 %slice-start.4 = ((s8[9437184]{0:T(1024)(128)(4,1)}), s8[4194304]{0:T(1024)(128)(4,1)S(1)}, s32[]{:S(2)}) async-start(s8[9437184]{0:T(1024)(128)(4,1)} %bitcast.158), calls=%async_computation.12 | async-start | bytes 8388608
  629.8 4.2 slice-start.5
  671.8 8.8 copy-start.6
  688.0 12.4 %copy-start.72 = (s32[1024]{0:T(1024)S(1)}, s32[1024]{0:T(1024)}, u32[]{:S(2)}) copy-start(s32[1024]{0:T(1024)} %copy-done.71) | copy-start | bytes 12292
  688.0 12.6 %copy-start.34 = (s32[262144]{0:T(1024)S(1)}, s32[262144]{0:T(1024)}, u32[]{:S(2)}) copy-start(s32[262144]{0:T(1024)} %copy-done.33) | copy-start | bytes 3145732
  700.6 8.5 copy-start.51
  700.7 8.5 copy-start.58
  700.7 8.5 copy-start.61
  (42 other events, 86.0 us)
Sparse Core Ops, SparseCore 0:
  10.8 56.7 all-gather.9
  70.4 53.1 all-gather.11
  126.4 53.0 all-gather.7
  182.2 53.0 all-gather.13
  237.9 62.5 all-gather.15
  303.1 62.3 all-gather.17
  368.3 62.3 all-gather.19
  671.9 556.0 all-reduce.11
where the time goes:
time: 1250 us; the launch traced here: 1240 us
  waiting for transfers between devices  647 us (52%)
  local copies, waits for them, and re-layouts  278 us (22%)
  matrix products  156 us (12%)
  blocking collectives  126 us (10%)
  between operations  16.8 us (1%)
  other arithmetic  16.7 us (1%)
    unnamed x9, waiting for transfers between devices  470 us
    unnamed x217, local copies, waits for them, and re-layouts  119 us
    all_gather x1, blocking collectives, local(): lax.all_gather(weight_proj, ('dp', 'fsdp'), axis=0, tiled=True)  70.2 us
    all_gather x1, waiting for transfers between devices, local(): lax.all_gather(weight_up, ('dp', 'fsdp'), axis=0, tiled=True)  56.8 us
    all_gather x1, waiting for transfers between devices, local(): lax.all_gather(weight_gate, ('dp', 'fsdp'), axis=0, tiled=True)  46 us
    psum x1, blocking collectives, local(): gain_whole, table_whole = lax.psum((gain_grads, table_flat), ('dp', 'fsdp'))  41.9 us
    reshape x7, local copies, waits for them, and re-layouts, local(): flat_rows.reshape(layout)  38 us
    all_gather x1, waiting for transfers between devices, local(): lax.all_gather(weight_down, ('dp', 'fsdp'), axis=0, tiled=True)  37.9 us
  transfers between devices with their start and end apart: 8, of which 6 were waited for; matrix products, arithmetic and copies ran while one was open for 16% of the time, Pallas kernels for 0%

commit v1 on v0

--- a/solution.py
+++ b/solution.py
@@ -1,6 +1,10 @@
+import functools
+
 import jax
 import jax.numpy as jnp
 from jax import lax
+from jax.experimental import pallas as pl
+from jax.experimental.pallas import tpu as pltpu
 from jax.sharding import PartitionSpec as P
 
 D = 768
@@ -355,6 +359,596 @@
     )
 
 
+WIDTHS = (3 * D, D + PROJ, 2 * FF, D)
+SHARE_ROWS = (24, 24, 24, 96)
+GATHER_STAGES = (
+    (0, 0, 768),
+    (0, 768, 768),
+    (0, 1536, 768),
+    (1, 0, 896),
+    (2, 0, 1536),
+    (2, 1536, 1536),
+    (2, 3072, 1536),
+    (2, 4608, 1536),
+    (3, 0, 384),
+    (3, 384, 384),
+)
+SCATTER_STAGES = (
+    (3, 0, 384),
+    (3, 384, 384),
+    (2, 0, 1536),
+    (2, 1536, 1536),
+    (2, 3072, 1536),
+    (2, 4608, 1536),
+    (1, 0, 896),
+    (0, 0, 768),
+    (0, 768, 768),
+    (0, 1536, 768),
+)
+MESH_ID = pl.DeviceIdType.MESH
+
+
+def remote(source, target, send_sem, recv_sem, device):
+    return pltpu.make_async_remote_copy(
+        src_ref=source,
+        dst_ref=target,
+        send_sem=send_sem,
+        recv_sem=recv_sem,
+        device_id=device,
+        device_id_type=MESH_ID,
+    )
+
+
+class Place:
+    def __init__(self):
+        self.dp = lax.axis_index("dp")
+        self.z = lax.axis_index("fsdp")
+        self.core = lax.rem(self.dp, 2)
+        self.xy = self.dp // 2
+        self.xy_x = self.xy + 1 - 2 * lax.rem(self.xy, 2)
+        self.xy_y = lax.rem(self.xy + 2, 4)
+        self.xy_d = 3 - self.xy
+        self.sib = self.dp + 1 - 2 * self.core
+        self.dp_x = 2 * self.xy_x + self.core
+        self.dp_y = 2 * self.xy_y + self.core
+        self.dp_d = 2 * self.xy_d + self.core
+        self.zs = [lax.rem(self.z + step, 4) for step in (1, 2, 3)]
+        self.to_sib = {"dp": self.sib}
+        self.to_x = {"dp": self.dp_x}
+        self.to_y = {"dp": self.dp_y}
+        self.to_z = [{"fsdp": other} for other in self.zs]
+
+    def barrier(self):
+        semaphore = pltpu.get_barrier_semaphore()
+        for device in [self.to_sib, self.to_x, self.to_y] + self.to_z:
+            pl.semaphore_signal(semaphore, inc=1, device_id=device, device_id_type=MESH_ID)
+        pl.semaphore_wait(semaphore, 6)
+
+
+class Gather:
+    def __init__(self, place, shards, whole, parts, sems):
+        self.place, self.shards, self.whole, self.parts = place, shards, whole, parts
+        (self.z_send, self.z_recv, self.send, self.recv) = sems
+        self.stages = GATHER_STAGES
+
+    @staticmethod
+    def scratch():
+        count = len(GATHER_STAGES)
+        dma = pltpu.SemaphoreType.DMA
+        return [dma((count, 3)), dma((count, 3)), dma((count, 9)), dma((count, 9))]
+
+    def z_copy(self, s, k):
+        array, first, width = self.stages[s]
+        place = self.place
+        columns = pl.ds(first, width)
+        if array == 3:
+            rows = pl.ds(pl.multiple_of(384 * place.dp + 96 * place.z, 96), 96)
+            target = self.whole[3].at[rows, columns]
+        else:
+            target = self.parts[array].at[k, :, columns]
+        return remote(
+            self.shards[array].at[:, columns],
+            target,
+            self.z_send.at[s, k],
+            self.z_recv.at[s, k],
+            place.to_z[k],
+        )
+
+    def block(self, s, dp, half=None):
+        array, first, width = self.stages[s]
+        count = 4 * SHARE_ROWS[array]
+        start = count * dp
+        if half is not None:
+            count = count // 2
+            start = start + half * count
+        return self.whole[array].at[
+            pl.ds(pl.multiple_of(start, 48), count), pl.ds(first, width)
+        ]
+
+    def hop(self, s, index):
+        place = self.place
+        dp, half, device = (
+            (place.dp, None, place.to_x),
+            (place.dp, None, place.to_y),
+            (place.dp_x, 0, place.to_y),
+            (place.dp_y, 1, place.to_x),
+            (place.dp, None, place.to_sib),
+            (place.dp_x, None, place.to_sib),
+            (place.dp_y, None, place.to_sib),
+            (place.dp_d, 0, place.to_sib),
+            (place.dp_d, 1, place.to_sib),
+        )[index]
+        block = self.block(s, dp, half)
+        return remote(block, block, self.send.at[s, index], self.recv.at[s, index], device)
+
+    def begin(self):
+        for s in range(len(self.stages)):
+            for k in range(3):
+                self.z_copy(s, k).start()
+
+    def spread(self, s):
+        array, first, width = self.stages[s]
+        place = self.place
+        columns = pl.ds(first, width)
+        for k in range(3):
+            self.z_copy(s, k).wait_recv()
+        if array == 3:
+            rows = pl.ds(pl.multiple_of(384 * place.dp + 96 * place.z, 96), 96)
+            self.whole[3][rows, columns] = self.shards[3][:, columns]
+        else:
+            pieces = []
+            for other in range(4):
+                piece = self.shards[array][:, columns]
+                for k in range(3):
+                    here = lax.rem(place.z + 3 - k, 4) == other
+                    piece = jnp.where(here, self.parts[array][k, :, columns], piece)
+                pieces.append(piece)
+            rows = pl.ds(pl.multiple_of(96 * place.dp, 96), 96)
+            self.whole[array][rows, columns] = jnp.concatenate(pieces, axis=0)
+        for index in (0, 1, 4):
+            self.hop(s, index).start()
+
+    def relay(self, s):
+        self.hop(s, 0).wait_recv()
+        self.hop(s, 2).start()
+        self.hop(s, 5).start()
+        self.hop(s, 1).wait_recv()
+        self.hop(s, 3).start()
+        self.hop(s, 6).start()
+
+    def hand_over(self, s):
+        self.hop(s, 2).wait_recv()
+        self.hop(s, 7).start()
+        self.hop(s, 3).wait_recv()
+        self.hop(s, 8).start()
+
+    def arrive(self, s):
+        for index in range(4, 9):
+            self.hop(s, index).wait_recv()
+
+    def step(self, t):
+        count = len(self.stages)
+        for lag, work in enumerate((self.spread, self.relay, self.hand_over, self.arrive)):
+            if 0 <= t - lag < count:
+                work(t - lag)
+
+    def finish(self):
+        for s in range(len(self.stages)):
+            for k in range(3):
+                self.z_copy(s, k).wait_send()
+            for index in range(9):
+                self.hop(s, index).wait_send()
+
+
+class Scatter:
+    def __init__(self, place, local, buffers, outputs, sems):
+        self.place, self.local, self.outputs = place, local, outputs
+        self.from_sib, self.from_x, self.from_y, self.z_out, self.z_in = (
+            buffers[0:4],
+            buffers[4:8],
+            buffers[8:12],
+            buffers[12:16],
+            buffers[16:20],
+        )
+        self.diag_x, self.diag_y = buffers[20:24], buffers[24:28]
+        self.send, self.recv = sems
+        self.stages = SCATTER_STAGES
+
+    @staticmethod
+    def scratch():
+        rows = [4 * count for count in SHARE_ROWS]
+        kind = jnp.bfloat16
+        shapes = [pltpu.VMEM((4, r, w), kind) for r, w in zip(rows, WIDTHS)]
+        shapes += [pltpu.VMEM((r, w), kind) for r, w in zip(rows, WIDTHS)] * 2
+        shapes += [pltpu.VMEM((4, r // 4, w), kind) for r, w in zip(rows, WIDTHS)]
+        shapes += [pltpu.VMEM((3, r // 4, w), kind) for r, w in zip(rows, WIDTHS)]
+        shapes += [pltpu.VMEM((r // 2, w), kind) for r, w in zip(rows, WIDTHS)] * 2
+        return shapes
+
+    @staticmethod
+    def semaphores():
+        count = len(SCATTER_STAGES)
+        dma = pltpu.SemaphoreType.DMA
+        return [dma((count, 8)), dma((count, 8))]
+
+    def copy(self, s, index):
+        array, first, width = self.stages[s]
+        place = self.place
+        columns = pl.ds(first, width)
+        half = 2 * SHARE_ROWS[array]
+        local = self.local(s)
+        if index == 0:
+            source = local.at[:, 1 - place.core]
+            target = self.from_sib[array].at[:, :, columns]
+            device = place.to_sib
+        elif index == 1:
+            source = local.at[place.xy_d, place.core, pl.ds(0, half)]
+            target = self.diag_x[array].at[:, columns]
+            device = place.to_x
+        elif index == 2:
+            source = local.at[place.xy_d, place.core, pl.ds(half, half)]
+            target = self.diag_y[array].at[:, columns]
+            device = place.to_y
+        elif index == 3:
+            source = local.at[place.xy_x, place.core]
+            target = self.from_x[array].at[:, columns]
+            device = place.to_x
+        elif index == 4:
+            source = local.at[place.xy_y, place.core]
+            target = self.from_y[array].at[:, columns]
+            device = place.to_y
+        else:
+            k = index - 5
+            source = self.z_out[array].at[place.zs[k], :, columns]
+            target = self.z_in[array].at[k, :, columns]
+            device = place.to_z[k]
+        return remote(source, target, self.send.at[s, index], self.recv.at[s, index], device)
+
+    def add(self, s, block, other, rows=None):
+        local = self.local(s)
+        here = (block, self.place.core) if rows is None else (block, self.place.core, rows)
+        total = local[here].astype(jnp.float32) + other.astype(jnp.float32)
+        local[here] = total.astype(jnp.bfloat16)
+
+    def begin(self, s):
+        self.copy(s, 0).start()
+
+    def pair(self, s):
+        array, first, width = self.stages[s]
+        place = self.place
+        columns = pl.ds(first, width)
+        self.copy(s, 0).wait_recv()
+        self.add(s, place.xy_d, self.from_sib[array][place.xy_d, :, columns])
+        self.copy(s, 1).start()
+        self.copy(s, 2).start()
+        for block in (place.xy_x, place.xy_y, place.xy):
+            self.add(s, block, self.from_sib[array][block, :, columns])
+
+    def cross(self, s):
+        array, first, width = self.stages[s]
+        place = self.place
+        columns = pl.ds(first, width)
+        half = 2 * SHARE_ROWS[array]
+        self.copy(s, 1).wait_recv()
+        self.add(s, place.xy_y, self.diag_x[array][:, columns], pl.ds(0, half))
+        self.copy(s, 4).start()
+        self.copy(s, 2).wait_recv()
+        self.add(s, place.xy_x, self.diag_y[array][:, columns], pl.ds(half, half))
+        self.copy(s, 3).start()
+
+    def square(self, s):
+        array, first, width = self.stages[s]
+        place = self.place
+        columns = pl.ds(first, width)
+        rows = SHARE_ROWS[array]
+        self.copy(s, 3).wait_recv()
+        self.copy(s, 4).wait_recv()
+        local = self.local(s)
+        for other in range(4):
+            piece = pl.ds(rows * other, rows)
+            total = (
+                local[place.xy, place.core, piece].astype(jnp.float32)
+                + self.from_x[array][piece, columns].astype(jnp.float32)
+                + self.from_y[array][piece, columns].astype(jnp.float32)
+            )
+            self.z_out[array][other, :, columns] = total.astype(jnp.bfloat16)
+        for k in range(3):
+            self.copy(s, 5 + k).start()
+
+    def settle(self, s):
+        array, first, width = self.stages[s]
+        columns = pl.ds(first, width)
+        total = self.z_out[array][self.place.z, :, columns].astype(jnp.float32)
+        for k in range(3):
+            self.copy(s, 5 + k).wait_recv()
+            total = total + self.z_in[array][k, :, columns].astype(jnp.float32)
+        self.outputs(s, total)
+
+    def step(self, t):
+        count = len(self.stages)
+        for lag, work in enumerate((self.begin, self.pair, self.cross, self.square, self.settle)):
+            if 0 <= t - lag < count:
+                work(t - lag)
+
+    def finish(self):
+        for s in range(len(self.stages)):
+            for index in range(8):
+                self.copy(s, index).wait_send()
+
+
+def gather_kernel(*refs):
+    shards, outs, whole, parts = refs[0:4], refs[4:8], refs[8:12], refs[12:15]
+    gather_sems, out_sem = refs[15:19], refs[19]
+    place = Place()
+    place.barrier()
+    gather = Gather(place, shards, whole, parts, gather_sems)
+    gather.begin()
+    count = len(GATHER_STAGES)
+    copies = []
+    for t in range(count + 3):
+        gather.step(t)
+        if t >= 3:
+            array, first, width = GATHER_STAGES[t - 3]
+            columns = pl.ds(first, width)
+            copies.append(
+                pltpu.make_async_copy(
+                    whole[array].at[:, columns], outs[array].at[:, columns], out_sem.at[t - 3]
+                )
+            )
+            copies[-1].start()
+    gather.finish()
+    for copy in copies:
+        copy.wait()
+
+
+def gather_all(shards):
+    rows = [32 * count for count in SHARE_ROWS]
+    kind = jnp.bfloat16
+    return pl.pallas_call(
+        gather_kernel,
+        out_shape=tuple(jax.ShapeDtypeStruct((r, w), kind) for r, w in zip(rows, WIDTHS)),
+        in_specs=[pl.BlockSpec(memory_space=pltpu.VMEM)] * 4,
+        out_specs=tuple(pl.BlockSpec(memory_space=pl.ANY) for _ in range(4)),
+        scratch_shapes=[pltpu.VMEM((r, w), kind) for r, w in zip(rows, WIDTHS)]
+        + [pltpu.VMEM((3, r, w), kind) for r, w in zip(SHARE_ROWS[:3], WIDTHS[:3])]
+        + Gather.scratch()
+        + [pltpu.SemaphoreType.DMA((len(GATHER_STAGES),))],
+        compiler_params=pltpu.CompilerParams(
+            collective_id=0, has_side_effects=True, vmem_limit_bytes=60 * 2**20
+        ),
+    )(*shards)
+
+
+def scatter_kernel(*refs):
+    grads, outs, local, buffers = refs[0:4], refs[4:8], refs[8:12], refs[12:40]
+    sems, in_sem = refs[40:42], refs[42]
+    place = Place()
+    copies = []
+    for s, (array, first, width) in enumerate(SCATTER_STAGES):
+        columns = pl.ds(first, width)
+        copies.append(
+            pltpu.make_async_copy(
+                grads[array].at[:, :, :, columns], local[array].at[:, :, :, columns], in_sem.at[s]
+            )
+        )
+        copies[-1].start()
+    place.barrier()
+
+    def part(s):
+        array, first, width = SCATTER_STAGES[s]
+        return local[array].at[:, :, :, pl.ds(first, width)]
+
+    def outputs(s, total):
+        array, first, width = SCATTER_STAGES[s]
+        outs[array][:, pl.ds(first, width)] = total
+
+    scatter = Scatter(place, part, buffers, outputs, sems)
+    for t in range(len(SCATTER_STAGES) + 4):
+        if t < len(SCATTER_STAGES):
+            copies[t].wait()
+        scatter.step(t)
+    scatter.finish()
+
+
+def scatter_all(grads):
+    kind = jnp.bfloat16
+    return pl.pallas_call(
+        scatter_kernel,
+        out_shape=tuple(
+            jax.ShapeDtypeStruct((r, w), jnp.float32) for r, w in zip(SHARE_ROWS, WIDTHS)
+        ),
+        in_specs=[pl.BlockSpec(memory_space=pl.ANY)] * 4,
+        out_specs=tuple(pl.BlockSpec(memory_space=pltpu.VMEM) for _ in range(4)),
+        scratch_shapes=[
+            pltpu.VMEM((4, 2, 4 * r, w), kind) for r, w in zip(SHARE_ROWS, WIDTHS)
+        ]
+        + Scatter.scratch()
+        + Scatter.semaphores()
+        + [pltpu.SemaphoreType.DMA((len(SCATTER_STAGES),))],
+        compiler_params=pltpu.CompilerParams(
+            collective_id=1, has_side_effects=True, vmem_limit_bytes=60 * 2**20
+        ),
+    )(*[grad.reshape(4, 2, 4 * r, w) for grad, r, w in zip(grads, SHARE_ROWS, WIDTHS)])
+
+
+def local_fast(
+    document_tokens,
+    document_lengths,
+    query_tokens,
+    query_lengths,
+    weight_query,
+    weight_key,
+    weight_value,
+    weight_out,
+    weight_gate,
+    weight_up,
+    weight_down,
+    weight_proj,
+    norm_gains,
+    rel_table,
+    document_cotangent,
+    query_cotangent,
+):
+    shards = (
+        jnp.concatenate(
+            [w.reshape(-1, D) for w in (weight_query, weight_key, weight_value)], axis=1
+        ),
+        jnp.concatenate([weight_out.reshape(-1, D), weight_proj.reshape(-1, PROJ)], axis=1),
+        jnp.stack(
+            [weight_gate.reshape(-1, 4, D), weight_up.reshape(-1, 4, D)], axis=2
+        ).reshape(-1, 2 * FF),
+        weight_down.reshape(-1, D),
+    )
+    qkv_mat, out_proj_mat, gate_up_mat, down_mat = gather_all(shards)
+    gains_all, table_all = (
+        lax.all_gather(norm_gains, "fsdp", axis=0, tiled=True),
+        lax.all_gather(rel_table, "fsdp", axis=0, tiled=True),
+    )
+    gain_rows = gains_all.astype(jnp.float32).reshape(3, D)
+    table_mat = table_all.reshape(BUCKETS, HEADS)
+    documents = document_tokens.shape[0]
+    queries_here = query_tokens.shape[0]
+    doc_rows = documents * DOC_LEN
+    doc_segments = segment_ids(document_lengths, DOC_LEN)
+    query_segments = segment_ids(query_lengths.reshape(queries_here, 1), QRY_LEN)
+    doc_allowed = doc_segments[:, None, :, None] == doc_segments[:, None, None, :]
+    query_allowed = query_segments[:, None, :, None] == query_segments[:, None, None, :]
+    doc_onehot = bucket_onehot(DOC_LEN)
+    query_onehot = bucket_onehot(QRY_LEN)
+    doc_bias = bias_rows(table_mat, doc_onehot, DOC_LEN)
+    query_bias = bias_rows(table_mat, query_onehot, QRY_LEN)
+    settings = [(doc_bias, doc_allowed, doc_onehot)]
+    settings.append((query_bias, query_allowed, query_onehot))
+
+    def split_blocks(matrix):
+        blocks_out = [matrix[0:DOC_LEN].reshape(1, DOC_LEN, HEADS, HEAD_DIM)]
+        blocks_out.append(matrix[doc_rows:].reshape(queries_here, QRY_LEN, HEADS, HEAD_DIM))
+        return blocks_out
+
+    query_mat, key_mat, value_mat = (qkv_mat[:, i * D : (i + 1) * D] for i in range(3))
+    out_mat, proj_mat = out_proj_mat[:, :D], out_proj_mat[:, D:]
+    inputs = jnp.concatenate(
+        [document_tokens.reshape(doc_rows, D), query_tokens.reshape(-1, D)], axis=0
+    )
+    residual_in = inputs.astype(jnp.float32)
+    normed_one, norm_one_back = jax.vjp(rms_norm, residual_in, gain_rows[0])
+    normed_one = normed_one.astype(jnp.bfloat16)
+    queries = jnp.dot(normed_one, query_mat, preferred_element_type=jnp.float32).astype(
+        jnp.bfloat16
+    )
+    key_rows = jnp.dot(normed_one, key_mat, preferred_element_type=jnp.float32).astype(jnp.bfloat16)
+    values = jnp.dot(normed_one, value_mat, preferred_element_type=jnp.float32).astype(jnp.bfloat16)
+    query_blocks = split_blocks(queries)
+    key_blocks = split_blocks(key_rows)
+    value_blocks = split_blocks(values)
+    contexts = []
+    log_totals = []
+    for query_block, key_block, value_block, setting in zip(
+        query_blocks, key_blocks, value_blocks, settings
+    ):
+        context_block, log_total = attend(
+            query_block, key_block, value_block, setting[0], setting[1]
+        )
+        contexts.append(context_block.reshape(-1, D))
+        log_totals.append(log_total)
+    context = jnp.concatenate(contexts, axis=0)
+    hidden = residual_in + jnp.dot(context, out_mat, preferred_element_type=jnp.float32)
+    normed_two, norm_two_back = jax.vjp(rms_norm, hidden, gain_rows[1])
+    normed_two = normed_two.astype(jnp.bfloat16)
+    def gated(mixed):
+        parts = [mixed[:, i * D : (i + 1) * D] for i in range(8)]
+        return jnp.concatenate([gated_unit(parts[2 * i], parts[2 * i + 1]) for i in range(4)], axis=1)
+
+    gate_up = jnp.dot(normed_two, gate_up_mat, preferred_element_type=jnp.float32)
+    inner, gated_back = jax.vjp(gated, gate_up)
+    inner = inner.astype(jnp.bfloat16)
+    final = hidden + jnp.dot(inner, down_mat, preferred_element_type=jnp.float32)
+    normed_three, norm_three_back = jax.vjp(rms_norm, final, gain_rows[2])
+    normed_three = normed_three.astype(jnp.bfloat16)
+    output = jnp.dot(normed_three, proj_mat, preferred_element_type=jnp.float32).astype(
+        jnp.bfloat16
+    )
+    cotangent = jnp.concatenate(
+        [document_cotangent.reshape(doc_rows, PROJ), query_cotangent.reshape(-1, PROJ)], axis=0
+    )
+    grad_final, grad_gain_three = norm_three_back(times_transposed(cotangent, proj_mat))
+    grad_ffn = grad_final.astype(jnp.bfloat16)
+    (grad_gate_up_f,) = gated_back(times_transposed(grad_ffn, down_mat))
+    grad_gate_up = grad_gate_up_f.astype(jnp.bfloat16)
+    grad_normed_two = times_transposed(grad_gate_up, gate_up_mat)
+    grad_hidden_part, grad_gain_two = norm_two_back(grad_normed_two)
+    grad_hidden = grad_final + grad_hidden_part
+    grad_branch = grad_hidden.astype(jnp.bfloat16)
+    grad_context = times_transposed(grad_branch, out_mat).astype(jnp.bfloat16)
+    table_grad = jnp.zeros((HEADS, BUCKETS), jnp.float32)
+    grad_query_parts = []
+    grad_key_parts = []
+    grad_value_parts = []
+    for query_block, key_block, value_block, setting, log_total, grad_block in zip(
+        query_blocks, key_blocks, value_blocks, settings, log_totals, split_blocks(grad_context)
+    ):
+        grad_q_block, grad_k_block, grad_v_block, grad_scores = attend_back(
+            query_block, key_block, value_block, setting[0], setting[1], log_total, grad_block
+        )
+        table_grad = table_grad + bias_grads(grad_scores, setting[2])
+        grad_query_parts.append(grad_q_block.reshape(-1, D))
+        grad_key_parts.append(grad_k_block.reshape(-1, D))
+        grad_value_parts.append(grad_v_block.reshape(-1, D))
+    grad_qkv = jnp.concatenate(
+        [jnp.concatenate(p, axis=0) for p in (grad_query_parts, grad_key_parts, grad_value_parts)],
+        axis=1,
+    )
+    grad_normed_one = times_transposed(grad_qkv, qkv_mat)
+    grad_input_part, grad_gain_one = norm_one_back(grad_normed_one)
+    grad_inputs = (grad_hidden + grad_input_part).astype(jnp.bfloat16)
+    summed = scatter_all(
+        (
+            outer_sum(normed_one, grad_qkv).astype(jnp.bfloat16),
+            jnp.concatenate(
+                [outer_sum(context, grad_branch), outer_sum(normed_three, cotangent)], axis=1
+            ).astype(jnp.bfloat16),
+            outer_sum(normed_two, grad_gate_up).astype(jnp.bfloat16),
+            outer_sum(inner, grad_ffn).astype(jnp.bfloat16),
+        )
+    )
+    mixed = summed[2].reshape(24, 4, 2, D)
+    shares = (
+        summed[0][:, :D].reshape(-1),
+        summed[0][:, D : 2 * D].reshape(-1),
+        summed[0][:, 2 * D :].reshape(-1),
+        summed[1][:, :D].reshape(-1),
+        mixed[:, :, 0].reshape(-1),
+        mixed[:, :, 1].reshape(-1),
+        summed[3].reshape(-1),
+        summed[1][:, D:].reshape(-1),
+    )
+    gain_grads = jnp.concatenate([grad_gain_one, grad_gain_two, grad_gain_three], axis=0)
+    table_flat = jnp.transpose(table_grad).reshape(-1)
+    gain_whole, table_whole = lax.psum((gain_grads, table_flat), ("dp", "fsdp"))
+    fsdp_index = lax.axis_index("fsdp")
+    fsdp_count = lax.axis_size("fsdp")
+    gain_share = 3 * D // fsdp_count
+    table_share = BUCKETS * HEADS // fsdp_count
+    own_gains = lax.dynamic_slice_in_dim(gain_whole, fsdp_index * gain_share, gain_share)
+    own_table = lax.dynamic_slice_in_dim(table_whole, fsdp_index * table_share, table_share)
+    return (
+        output[:doc_rows].reshape(documents, DOC_LEN, PROJ),
+        output[doc_rows:].reshape(queries_here, QRY_LEN, PROJ),
+        grad_inputs[:doc_rows].reshape(documents, DOC_LEN, D),
+        grad_inputs[doc_rows:].reshape(queries_here, QRY_LEN, D),
+        shares[0],
+        shares[1],
+        shares[2],
+        shares[3],
+        shares[4],
+        shares[5],
+        shares[6],
+        shares[7],
+        own_gains,
+        own_table,
+    )
+
+
 def solution(mesh):
     placed = (
         P(("dp", "fsdp"), None, None),
@@ -375,7 +969,7 @@
         P(("dp", "fsdp"), None, None),
     )
     return jax.shard_map(
-        local,
+        local_fast if (mesh.shape["dp"], mesh.shape["fsdp"]) == (8, 4) else local,
         mesh=mesh,
         in_specs=placed,
         out_specs=(

time: 1250 us -> 596 us (0.48)
  waiting for transfers between devices: 647 us -> 0 us
  Pallas kernels: 0 us -> 188 us
  local copies, waits for them, and re-layouts: 278 us -> 127 us
  blocking collectives: 126 us -> 52.6 us
  other arithmetic: 16.7 us -> 53.7 us
  between operations: 16.8 us -> 3.35 us
    unnamed x9 -> x0, waiting for transfers between devices: 470 us -> none
    pallas_call x0 -> x2, Pallas kernels: none -> 188 us  [the longest x1 94.9 us: scatter_all(): pl.pallas_call(scatter_kernel, out_shape=tuple((jax.ShapeDtypeStruct((r,...]
    all_gather x7 -> x0, waiting for transfers between devices: 177 us -> none  [the longest x1 56.8 us: local(): lax.all_gather(weight_up, ('dp', 'fsdp'), axis=0, tiled=True)]
    unnamed x217 -> x137, local copies, waits for them, and re-layouts: 119 us -> 44.4 us
    all_gather x1 -> x0, blocking collectives: 70.2 us -> none  [local(): lax.all_gather(weight_proj, ('dp', 'fsdp'), axis=0, tiled=True)]
    reshape x28 -> x25, local copies, waits for them, and re-layouts: 93.2 us -> 27.6 us  [the longest x2 5.77 us: local_fast(): contexts.append(context_block.reshape(-1, D))]
    mul x0 -> x2, other arithmetic: none -> 16.8 us  [gated_unit(): return jax.nn.gelu(gate_in, approximate=True) * upper_in]
    dot_general x8 -> x5, matrix products: 36.3 us -> 43.9 us  [outer_sum(): lax.dot_general(left_rows, right_rows, (((0,), (0,)), ((), ())), preferre...]
  transfers between devices with their start and end apart: 8 -> 0, of which waited for: 6 -> 0; matrix products, arithmetic and copies ran while one was open for 16% -> 0% of each run, Pallas kernels for 0% -> 0%
where the time goes in v1:
time: 596 us; the launch traced here: 590 us
  Pallas kernels  188 us (32%)
  matrix products  165 us (28%)
  local copies, waits for them, and re-layouts  127 us (21%)
  other arithmetic  53.7 us (9%)
  blocking collectives  52.6 us (9%)
    pallas_call x1, Pallas kernels, scatter_all(): pl.pallas_call(scatter_kernel, out_shape=tuple((jax.ShapeDtypeStruct((r,...  94.9 us
    pallas_call x1, Pallas kernels, gather_all(): pl.pallas_call(gather_kernel, out_shape=tuple((jax.ShapeDtypeStruct((r, w...  93.4 us
    unnamed x137, local copies, waits for them, and re-layouts  44.4 us
    dot_general x5, matrix products, outer_sum(): lax.dot_general(left_rows, right_rows, (((0,), (0,)), ((), ())), preferre...  43.9 us
    dot_general x5, matrix products, times_transposed(): lax.dot_general(left_rows, matrix, (((1,), (1,)), ((), ())), preferred_el...  42 us
    psum x1, blocking collectives, local_fast(): gain_whole, table_whole = lax.psum((gain_grads, table_flat), ('dp', 'fsdp'))  38.9 us
    reshape x2, local copies, waits for them, and re-layouts, bias_rows(): return rel_bias.reshape(1, HEADS, length, length)  23.5 us
    mul x2, other arithmetic, gated_unit(): return jax.nn.gelu(gate_in, approximate=True) * upper_in  16.8 us

profile of v1, /device:TPU:0, one launch (start us, length us, event | category | flops | bytes accessed | tf_op | source)
XLA Modules:
  0.0 590.0 jit_solution(11891787434210209048)
XLA Ops:
  0.7 1.3 dynamic-slice
  5.0 1.6 fusion.36
  8.2 13.7 %all-reduce.11 = (bf16[2304]{0:T(1024)(128)(2,1)S(1)}, bf16[384]{0:T(512)(128)(2,1)S(1)}) all-reduce(bf16[2304]{0:T(1024)(128)(2,1)S(1)} %dynamic-update-slice, bf16[384]{0:T(512)(128)(2,1)S(1)} %dynamic-update-slice.1), channel_id=1, replica_groups=mesh['dp'=8,'fsdp'=4] {'fsdp'}, use_global_device_ids=true, to_apply=%add.8 | all-reduce | flops 2688 | bytes 10752
  27.0 1.3 pad_maximum_fusion.13.refs_1_
  34.1 6.1 %fusion.1 = f32[12,262144]{1,0:T(8,128)S(1)} fusion(bf16[32,12]{1,0:T(8,128)(2,1)S(1)} %reshape.631, s32[262144]{0:T(1024)S(1)} %fusion.57), kind=kOutput, calls=%fused_computation.2 | convolution fusion | flops 209715200 | bytes 13632256 | tf_op jit(solution)/shard_map/dot_general | solution.py:104
  40.3 19.1 %copy.135 = f32[2,8,512,512]{3,2,1,0:T(8,128)} copy(f32[2,8,512,512]{3,1,2,0:T(8,128)S(1)} %bitcast.138) | data formatting | bytes 33554432
  59.4 10.6 %slice.168 = f32[12,512,512]{2,1,0:T(8,128)} slice(f32[16,512,512]{2,1,0:T(8,128)} %bitcast.139), slice={[0:12], [0:512], [0:512]} | slice | bytes 25165824 | tf_op jit(solution)/shard_map/reshape | solution.py:107
  70.0 12.9 %copy.79 = f32[12,512,512]{1,2,0:T(8,128)} copy(f32[12,512,512]{2,1,0:T(8,128)} %slice.168) | data formatting | bytes 25165824 | tf_op jit(solution)/shard_map/reshape | solution.py:107
  82.9 93.4 %shard_map.263 = (bf16[768,2304]{1,0:T(8,128)(2,1)}, bf16[768,896]{1,0:T(8,128)(2,1)}, bf16[768,6144]{1,0:T(8,128)(2,1)}, bf16[3072,768]{1,0:T(8,128)(2,1)}) custom-call(bf16[24,2304]{1,0:T(8,128)(2,1)} %pad_maximum_fusion.12.refs_0_, bf16[24,896]{1,0:T(8,128)(2,1)} %pad_maximum_fusion.13.refs_1_, bf16[24,6144]{1,0:T(8,128)(2,1)} %reshape.626.refs_2_, ...), custom_call_target="tpu_custom_call" | custom-call | tf_op jit(solution)/shard_map/pallas_call | solution.py:707
  176.3 2.5 convolution_convert_fusion.5
  178.9 3.2 convolution_convert_fusion.6
  183.0 6.3 %fusion.116 = (f32[12,512]{1,0:T(8,128)S(1)}, f32[12,512,512]{1,2,0:T(8,128)S(1)}) fusion(f32[12,512,512]{1,2,0:T(8,128)} %copy.79, bf16[512,12,64]{0,2,1:T(8,128)(2,1)S(1)} %bitcast.149, bf16[512,12,64]{0,2,1:T(8,128)(2,1)S(1)} %bitcast.141, pred[512,512]{0,1:T(8,128)(4,1)S(1)} %broadcast_compare_fusion), kind=kOutput, calls=%fused_computation.204 | convolution fusion | flops 412084224 | bytes 27025408 | tf_op jit(solution)/shard_map/bqhd,bkhd->bhqk/dot_general | solution.py:112
  189.3 1.9 exponential_reduce_fusion
  191.3 3.5 convolution_convert_fusion.7
  194.8 3.0 fusion.42
  198.4 1.5 copy.87
  200.0 2.2 reshape.710
  202.2 1.7 copy.84
  204.6 1.8 copy.85
  206.4 1.9 fusion.115
  208.8 1.3 fusion.48
  210.2 2.7 copy.116
  212.9 3.0 reshape.705
  215.9 4.4 multiply_reduce_fusion.6
  220.3 10.9 %fusion.106 = f32[768,6144]{1,0:T(8,128)S(1)} fusion(bf16[768,6144]{1,0:T(8,128)(2,1)} %get-tuple-element.24, f32[768,768]{1,0:T(8,128)} %get-tuple-element.66, f32[768]{0:T(1024)S(1)} %get-tuple-element.59, f32[768]{0:T(1024)S(1)} %fusion.98), kind=kOutput, calls=%fused_computation.198 | convolution fusion | flops 7249526784 | bytes 30676992 | tf_op jit(solution)/shard_map/dot_general | solution.py:862
  231.2 3.5 multiply_convert_fusion.5
  234.9 8.0 %multiply_reduce_fusion.5 = (f32[768]{0:T(1024)S(1)}, f32[768,768]{1,0:T(8,128)S(1)}) fusion(f32[768,768]{1,0:T(8,128)S(1)} %copy-done.23, bf16[3072,768]{1,0:T(8,128)(2,1)} %get-tuple-element.25, bf16[768,768]{1,0:T(8,128)(2,1)S(1)} %get-tuple-element.48, bf16[768,768]{1,0:T(8,128)(2,1)S(1)} %get-tuple-element.49, ...), kind=kOutput, calls=%fused_computation.72 | convolution fusion | flops 3644521728 | bytes 14158848 | tf_op jit(solution)/shard_map/dot_general | solution.py:865
  242.9 1.7 multiply_reduce_fusion.1
  244.7 2.5 add_add_fusion.2
  247.2 9.1 %convolution_convert_fusion.2 = bf16[3072,768]{1,0:T(8,128)(2,1)} fusion(bf16[768,768]{1,0:T(8,128)(2,1)} %copy-done.29, bf16[768,768]{1,0:T(8,128)(2,1)} %copy-done.30, bf16[768,768]{1,0:T(8,128)(2,1)} %copy-done.31, bf16[768,768]{1,0:T(8,128)(2,1)} %copy-done.28, f32[768,768]{1,0:T(8,128)} %get-tuple-element.51), kind=kOutput, calls=%fused_computation.14 | convolution fusion | flops 3645702144 | bytes 11796480 | tf_op jit(solution)/shard_map/dot_general | solution.py:57
  256.3 1.9 convolution_convert_fusion.15
  258.2 1.8 convolution_convert_fusion.14
  261.3 8.6 %fusion.72 = f32[768,3072]{1,0:T(8,128)} fusion(bf16[3072,768]{1,0:T(8,128)(2,1)} %get-tuple-element.25, f32[768,768]{1,0:T(8,128)S(1)} %copy-done.6), kind=kOutput, calls=%fused_computation.143 | convolution fusion | flops 3624468480 | bytes 16515072 | tf_op jit(solution)/shard_map/dot_general | solution.py:63
  269.9 3.9 slice_multiply_fusion.2
  273.8 12.9 %slice_multiply_fusion.3 = (f32[768,768]{1,0:T(8,128)}, f32[768,768]{1,0:T(8,128)}, f32[768,768]{1,0:T(8,128)}, f32[768,768]{1,0:T(8,128)}, f32[768,768]{1,0:T(8...) fusion(f32[768,3072]{1,0:T(8,128)} %fusion.72, f32[768,6144]{1,0:T(8,128)S(1)} %fusion.106), kind=kLoop, calls=%fused_computation.82 | loop fusion | flops 50724864 | bytes 44826624 | tf_op jit(solution)/shard_map/transpose(jvp())/mul | solution.py:30
  286.7 7.4 %add_convert_fusion = bf16[768,6144]{1,0:T(8,128)(2,1)S(1)} fusion(f32[768,768]{1,0:T(8,128)} %get-tuple-element.44, f32[768,768]{1,0:T(8,128)} %get-tuple-element.45, f32[768,768]{1,0:T(8,128)} %get-tuple-element.43, f32[768,768]{1,0:T(8,128)} %get-tuple-element.46, f32[768,768]{1,0:T(8,128)} %get-tuple-element.42, f32[768,768]{1,0:T(8,128)} %slice_multiply_fusion.2, ...), kind=kLoop, calls=%fused_computation.3 | loop fusion | flops 37748736 | bytes 28311552 | tf_op jit(solution)/shard_map/convert_element_type | solution.py:877
  294.2 13.0 %multiply_reduce_fusion.2 = (f32[768]{0:T(1024)S(1)}, f32[768]{0:T(1024)S(1)}, f32[768,768]{1,0:T(8,128)}) fusion(f32[768,768]{1,0:T(8,128)} %get-tuple-element.66, f32[768]{0:T(1024)S(1)} %fusion.98, f32[768]{0:T(1024)S(1)} %get-tuple-element.59, bf16[768,6144]{1,0:T(8,128)(2,1)S(1)} %add_convert_fusion, bf16[768,6144]{1,0:T(8,128)(2,1)} %get-tuple-element.24), kind=kOutput, calls=%fused_computation.68 | convolution fusion | flops 7251294208 | bytes 23605248 | tf_op jit(solution)/shard_map/dot_general | solution.py:63
  307.2 12.2 %convolution_convert_fusion = bf16[768,6144]{1,0:T(8,128)(2,1)} fusion(bf16[768,6144]{1,0:T(8,128)(2,1)S(1)} %add_convert_fusion, f32[768,768]{1,0:T(8,128)} %get-tuple-element.66, f32[768]{0:T(1024)S(1)} %get-tuple-element.59, f32[768]{0:T(1024)S(1)} %fusion.98), kind=kOutput, calls=%fused_computation.11 | convolution fusion | flops 7254245376 | bytes 21239808 | tf_op jit(solution)/shard_map/dot_general | solution.py:57
  319.5 2.4 fusion.33
  321.9 4.0 convolution_convert_fusion.4
  329.1 2.9 fusion.45
  332.1 2.8 reshape.712
  334.9 2.9 copy.93
  337.7 2.4 fusion.51
  341.9 1.2 fusion.50
  343.1 1.4 fusion.49
  345.9 2.0 copy.117
  347.9 1.9 reshape.706
  350.7 1.8 reshape.707
  352.6 2.1 copy.119
  354.7 1.8 reshape.708
  356.6 6.1 %multiply_reduce_fusion = (f32[12,512]{1,0:T(8,128)S(1)}, f32[12,512,512]{1,2,0:T(8,128)S(1)}) fusion(f32[12,512,512]{1,2,0:T(8,128)} %copy-done, f32[12,512]{1,0:T(8,128)S(1)} %copy-done.33, bf16[512,12,64]{0,2,1:T(8,128)(2,1)S(1)} %bitcast.148, bf16[512,12,64]{0,2,1:T(8,128)(2,1)S(1)} %bitcast.146), kind=kOutput, calls=%fused_computation.7 | convolution fusion | flops 412084224 | bytes 26787840 | tf_op jit(solution)/shard_map/bqhd,bkhd->bhqk/dot_general | solution.py:131
  362.6 6.9 %multiply_convert_fusion = bf16[12,512,512]{1,2,0:T(8,128)(2,1)S(1)} fusion(f32[12,512,512]{1,2,0:T(8,128)S(1)} %get-tuple-element.74, f32[12,512,512]{1,2,0:T(8,128)} %copy-done, f32[12,512]{1,0:T(8,128)S(1)} %get-tuple-element.73, f32[12,512]{1,0:T(8,128)S(1)} %copy-done.33), kind=kLoop, calls=%fused_computation.6 | loop fusion | flops 12582912 | bytes 31506432 | tf_op jit(solution)/shard_map/convert_element_type | solution.py:141
  369.6 2.0 convolution_convert_fusion.10
  375.3 14.7 %fusion.8 = (f32[768]{0:T(1024)S(1)}, f32[768]{0:T(1024)S(1)}, f32[768,768]{1,0:T(8,128)}) fusion(f32[768]{0:T(1024)S(1)} %copy-done.56, bf16[256,768]{1,0:T(8,128)(2,1)S(1)} %bitcast.171, bf16[512,768]{1,0:T(8,128)(2,1)S(1)} %bitcast.162, f32[768]{0:T(1024)S(1)} %copy-done.54, bf16[768,2304]{1,0:T(8,128)(2,1)S(1)} %copy-done.59, ...), kind=kOutput, calls=%fused_computation.37 | convolution fusion | flops 2745039360 | bytes 10629120 | tf_op jit(solution)/shard_map/dot_general | solution.py:63
  389.9 19.6 %convolution_convert_fusion.1 = bf16[768,2304]{1,0:T(8,128)(2,1)} fusion(bf16[256,768]{0,1:T(8,128)(2,1)S(1)} %copy-done.41, bf16[512,768]{0,1:T(8,128)(2,1)S(1)} %bitcast.178, bf16[256,768]{0,1:T(8,128)(2,1)S(1)} %copy-done.40, bf16[512,768]{0,1:T(8,128)(2,1)S(1)} %bitcast.180, bf16[256,768]{0,1:T(8,128)(2,1)S(1)} %copy-done.39, ...), kind=kOutput, calls=%fused_computation.13 | convolution fusion | flops 2745040896 | bytes 8263680 | tf_op jit(solution)/shard_map/dot_general | solution.py:57
  409.6 94.9 %shard_map.264 = (f32[24,2304]{1,0:T(8,128)}, f32[24,896]{1,0:T(8,128)}, f32[24,6144]{1,0:T(8,128)}, f32[96,768]{1,0:T(8,128)}) custom-call(bf16[4,2,96,2304]{3,2,1,0:T(8,128)(2,1)} %bitcast.155, bf16[4,2,96,896]{3,2,1,0:T(8,128)(2,1)} %pad_maximum_fusion.1.refs_1_, bf16[4,2,96,6144]{3,2,1,0:T(8,128)(2,1)} %bitcast.143, bf16[4,2,384,768]{3,2,1,0:T(8,128)(2,1)} %bitcast.151), custom_call_target="tpu_custom_call" | custom-call | tf_op jit(solution)/shard_map/pallas_call | solution.py:755
  504.5 2.5 fusion.35
  507.0 8.9 %copy.107 = bf16[12,512,512]{2,1,0:T(8,128)(2,1)} copy(bf16[12,512,512]{1,2,0:T(8,128)(2,1)} %copy-done.1) | data formatting | bytes 12582912 | tf_op jit(solution)/shard_map/convert_element_type | solution.py:141
  522.1 1.3 fusion.112
  523.4 6.8 %pad.60 = bf16[16,512,512]{2,1,0:T(8,128)(2,1)} pad(bf16[12,512,512]{2,1,0:T(8,128)(2,1)} %copy.107, bf16[]{:T(256)} %constant.110), padding=0_4x0_0x0_0 | pad | bytes 14680066
  530.2 11.4 %copy.136 = bf16[2,8,512,512]{3,1,2,0:T(8,128)(2,1)} copy(bf16[2,8,512,512]{3,2,1,0:T(8,128)(2,1)} %bitcast.140) | data formatting | bytes 16777216
  541.6 7.9 %fusion.56 = f32[32,12]{0,1:T(8,128)S(1)} fusion(bf16[12,262144]{1,0:T(8,128)(2,1)} %bitcast.144, s32[262144]{0:T(1024)S(1)} %copy-done.18, f32[12,32]{1,0:T(8,128)S(1)} %convolution_reduce_fusion), kind=kOutput, calls=%fused_computation.122 | convolution fusion | flops 209715584 | bytes 7343104 | tf_op jit(solution)/shard_map/dot_general | solution.py:159
  549.7 38.9 %all-reduce.10 = (f32[2304]{0:T(1024)S(1)}, f32[384]{0:T(512)S(1)}) all-reduce(f32[2304]{0:T(1024)S(1)} %pad_maximum_fusion.14, f32[384]{0:T(512)S(1)} %reshape.663), channel_id=1, replica_groups=mesh['dp'=8,'fsdp'=4] {'dp','fsdp'}, use_global_device_ids=true, to_apply=%region_17.18 | all-reduce | flops 2688 | bytes 21504 | tf_op jit(solution)/shard_map/psum | solution.py:927
  (212 shorter events, 36.6 us)
Async XLA Ops:
  0.6 28.8 %copy-start.45 = (bf16[73728]{0:T(1024)(128)(2,1)S(1)}, bf16[73728]{0:T(1024)(128)(2,1)}, u32[]{:S(2)}) copy-start(bf16[73728]{0:T(1024)(128)(2,1)} %param.25) | copy-start | bytes 442372
  0.7 28.8 %copy-start.44 = (bf16[73728]{0:T(1024)(128)(2,1)S(1)}, bf16[73728]{0:T(1024)(128)(2,1)}, u32[]{:S(2)}) copy-start(bf16[73728]{0:T(1024)(128)(2,1)} %param.24) | copy-start | bytes 442372
  5.0 26.0 %copy-start.46 = (bf16[73728]{0:T(1024)(128)(2,1)S(1)}, bf16[73728]{0:T(1024)(128)(2,1)}, u32[]{:S(2)}) copy-start(bf16[73728]{0:T(1024)(128)(2,1)} %param.26) | copy-start | bytes 442372
  6.6 15.4 %copy-start.51 = (f32[768]{0:T(1024)}, f32[768]{0:T(1024)S(1)}, u32[]{:S(2)}) copy-start(f32[768]{0:T(1024)S(1)} %fusion.36) | copy-start | bytes 9220
  22.0 169.2 %copy-start.53 = (f32[768]{0:T(1024)}, f32[768]{0:T(1024)S(1)}, u32[]{:S(2)}) copy-start(f32[768]{0:T(1024)S(1)} %get-tuple-element.60) | copy-start | bytes 9220
  22.1 169.2 %copy-start.55 = (f32[768]{0:T(1024)}, f32[768]{0:T(1024)S(1)}, u32[]{:S(2)}) copy-start(f32[768]{0:T(1024)S(1)} %get-tuple-element.76) | copy-start | bytes 9220
  22.4 6.0 %copy-start.57 = (s32[1024]{0:T(1024)}, s32[1024]{0:T(1024)S(1)}, u32[]{:S(2)}) copy-start(s32[1024]{0:T(1024)S(1)} %fusion.95) | copy-start | bytes 12292
  34.1 6.1 %copy-start.17 = (s32[262144]{0:T(1024)}, s32[262144]{0:T(1024)S(1)}, u32[]{:S(2)}) copy-start(s32[262144]{0:T(1024)S(1)} %fusion.57) | copy-start | bytes 3145732
  70.0 106.3 %copy-start.20 = (bf16[1,512,768]{2,1,0:T(8,128)(2,1)S(1)}, bf16[1,512,768]{2,1,0:T(8,128)(2,1)}, u32[]{:S(2)}) copy-start(bf16[1,512,768]{2,1,0:T(8,128)(2,1)} %param.16) | copy-start | bytes 2359300
  70.0 106.3 %copy-start.26 = (bf16[8,32,768]{2,1,0:T(8,128)(2,1)S(1)}, bf16[8,32,768]{2,1,0:T(8,128)(2,1)}, u32[]{:S(2)}) copy-start(bf16[8,32,768]{2,1,0:T(8,128)(2,1)} %param.18) | copy-start | bytes 1179652
  178.8 3.3 copy-start.25
  178.9 4.1 copy-start.2
  183.0 6.4 %copy-start.10 = (bf16[512,768]{0,1:T(8,128)(2,1)}, bf16[512,768]{0,1:T(8,128)(2,1)S(1)}, u32[]{:S(2)}) copy-start(bf16[512,768]{0,1:T(8,128)(2,1)S(1)} %slice.145) | copy-start | bytes 2359300
  189.3 5.5 copy-start
  191.3 3.6 copy-start.32
  199.9 8.9 %copy-start.12 = (bf16[8,32,12,64]{3,1,2,0:T(8,128)(2,1)}, bf16[8,32,12,64]{3,1,2,0:T(8,128)(2,1)S(1)}, u32[]{:S(2)}) copy-start(bf16[8,32,12,64]{3,1,2,0:T(8,128)(2,1)S(1)} %copy.87) | copy-start | bytes 1179652
  199.9 4.0 slice-start.3
  204.6 1.8 copy-start.36
  204.6 1.8 copy-start.47
  210.2 5.8 copy-start.21
  231.2 3.6 copy-start.23
  234.8 8.1 %copy-start.28 = (bf16[768,768]{1,0:T(8,128)(2,1)}, bf16[768,768]{1,0:T(8,128)(2,1)S(1)}, u32[]{:S(2)}) copy-start(bf16[768,768]{1,0:T(8,128)(2,1)S(1)} %get-tuple-element.47) | copy-start | bytes 3538948
  234.8 8.1 %copy-start.29 = (bf16[768,768]{1,0:T(8,128)(2,1)}, bf16[768,768]{1,0:T(8,128)(2,1)S(1)}, u32[]{:S(2)}) copy-start(bf16[768,768]{1,0:T(8,128)(2,1)S(1)} %get-tuple-element.48) | copy-start | bytes 3538948
  234.8 8.1 %copy-start.30 = (bf16[768,768]{1,0:T(8,128)(2,1)}, bf16[768,768]{1,0:T(8,128)(2,1)S(1)}, u32[]{:S(2)}) copy-start(bf16[768,768]{1,0:T(8,128)(2,1)S(1)} %get-tuple-element.49) | copy-start | bytes 3538948
  234.8 8.1 %copy-start.31 = (bf16[768,768]{1,0:T(8,128)(2,1)}, bf16[768,768]{1,0:T(8,128)(2,1)S(1)}, u32[]{:S(2)}) copy-start(bf16[768,768]{1,0:T(8,128)(2,1)S(1)} %get-tuple-element.50) | copy-start | bytes 3538948
  234.8 8.1 %copy-start.48 = (bf16[1,512,128]{2,1,0:T(8,128)(2,1)S(1)}, bf16[1,512,128]{2,1,0:T(8,128)(2,1)}, u32[]{:S(2)}) copy-start(bf16[1,512,128]{2,1,0:T(8,128)(2,1)} %param.30) | copy-start | bytes 393220
  234.8 8.1 %copy-start.50 = (bf16[8,32,128]{2,1,0:T(8,128)(2,1)S(1)}, bf16[8,32,128]{2,1,0:T(8,128)(2,1)}, u32[]{:S(2)}) copy-start(bf16[8,32,128]{2,1,0:T(8,128)(2,1)} %param.31) | copy-start | bytes 196612
  256.3 5.0 copy-start.6
  307.2 12.3 %copy-start.7 = (f32[768,768]{1,0:T(8,128)S(1)}, f32[768,768]{1,0:T(8,128)}, u32[]{:S(2)}) copy-start(f32[768,768]{1,0:T(8,128)} %get-tuple-element.51) | copy-start | bytes 7077892
  307.2 12.3 %copy-start.24 = (f32[768,768]{1,0:T(8,128)S(1)}, f32[768,768]{1,0:T(8,128)}, u32[]{:S(2)}) copy-start(f32[768,768]{1,0:T(8,128)} %get-tuple-element.66) | copy-start | bytes 7077892
  319.5 9.6 %slice-start = ((s8[12582912]{0:T(1024)(128)(4,1)}), s8[4194304]{0:T(1024)(128)(4,1)S(1)}, s32[]{:S(2)}) async-start(s8[12582912]{0:T(1024)(128)(4,1)} %bitcast.136), calls=%async_computation | async-start | bytes 8388608
  319.5 9.6 %slice-start.1 = ((s8[12582912]{0:T(1024)(128)(4,1)}), s8[4194304]{0:T(1024)(128)(4,1)S(1)}, s32[]{:S(2)}) async-start(s8[12582912]{0:T(1024)(128)(4,1)} %bitcast.136), calls=%async_computation.1 | async-start | bytes 8388608
  321.8 4.0 copy-start.4
  321.8 4.0 copy-start.34
  321.9 4.0 copy-start.38
  325.9 3.2 slice-start.2
  327.0 2.1 copy-start.33
  329.1 3.0 copy-start.8
  334.9 5.3 copy-start.13
  337.7 2.5 copy-start.14
  340.7 1.1 copy-start.15
  340.8 2.4 copy-start.16
  343.1 2.5 copy-start.58
  345.7 4.0 copy-start.19
  352.6 4.0 copy-start.9
  362.6 7.0 %copy-start.11 = (bf16[512,768]{0,1:T(8,128)(2,1)S(1)}, bf16[512,768]{0,1:T(8,128)(2,1)}, u32[]{:S(2)}) copy-start(bf16[512,768]{0,1:T(8,128)(2,1)} %copy-done.10) | copy-start | bytes 2359300
  369.6 2.6 copy-start.1
  369.6 2.6 copy-start.3
  372.3 1.2 copy-start.22
  372.3 1.2 copy-start.27
  372.3 1.5 copy-start.35
  372.3 1.6 copy-start.39
  372.3 1.7 copy-start.40
  372.3 1.8 copy-start.41
  372.3 1.8 copy-start.54
  372.3 1.8 copy-start.56
  372.3 3.0 copy-start.59
  409.5 95.0 %copy-start.52 = (f32[768]{0:T(1024)S(1)}, f32[768]{0:T(1024)}, u32[]{:S(2)}) copy-start(f32[768]{0:T(1024)} %copy-done.51) | copy-start | bytes 9220
  409.5 95.0 %copy-start.5 = (f32[768,768]{1,0:T(8,128)S(1)}, f32[768,768]{1,0:T(8,128)}, u32[]{:S(2)}) copy-start(f32[768,768]{1,0:T(8,128)} %copy-done.4) | copy-start | bytes 7077892
  507.0 9.0 %copy-start.43 = (f32[24,2304]{1,0:T(8,128)S(1)}, f32[24,2304]{1,0:T(8,128)}, u32[]{:S(2)}) copy-start(f32[24,2304]{1,0:T(8,128)} %get-tuple-element.26) | copy-start | bytes 663556
  507.0 9.6 %copy-start.49 = (f32[24,896]{1,0:T(8,128)S(1)}, f32[24,896]{1,0:T(8,128)}, u32[]{:S(2)}) copy-start(f32[24,896]{1,0:T(8,128)} %get-tuple-element.27) | copy-start | bytes 258052
  507.0 12.2 %copy-start.42 = (f32[96,768]{1,0:T(8,128)S(1)}, f32[96,768]{1,0:T(8,128)}, u32[]{:S(2)}) copy-start(f32[96,768]{1,0:T(8,128)} %get-tuple-element.29) | copy-start | bytes 884740
  516.0 5.6 copy-start.37
  530.2 11.4 %copy-start.18 = (s32[262144]{0:T(1024)S(1)}, s32[262144]{0:T(1024)}, u32[]{:S(2)}) copy-start(s32[262144]{0:T(1024)} %copy-done.17) | copy-start | bytes 3145732

commit v2 on v0

--- a/solution.py
+++ b/solution.py
@@ -1,6 +1,8 @@
 import jax
 import jax.numpy as jnp
 from jax import lax
+from jax.experimental import pallas as pl
+from jax.experimental.pallas import tpu as pltpu
 from jax.sharding import PartitionSpec as P
 
 D = 768
@@ -355,6 +357,1293 @@
     )
 
 
+WIDTHS = (3 * D, D + PROJ, 2 * FF, D)
+SHARE_ROWS = (24, 24, 24, 96)
+GATHER_STAGES = (
+    (0, 0, 768),
+    (0, 768, 768),
+    (0, 1536, 768),
+    (1, 0, 896),
+    (2, 0, 1536),
+    (2, 1536, 1536),
+    (2, 3072, 1536),
+    (2, 4608, 1536),
+    (3, 0, 384),
+    (3, 384, 384),
+)
+MESH_ID = pl.DeviceIdType.MESH
+
+
+def remote(source, target, send_sem, recv_sem, device):
+    return pltpu.make_async_remote_copy(
+        src_ref=source,
+        dst_ref=target,
+        send_sem=send_sem,
+        recv_sem=recv_sem,
+        device_id=device,
+        device_id_type=MESH_ID,
+    )
+
+
+class Place:
+    def __init__(self):
+        self.dp = lax.axis_index("dp")
+        self.z = lax.axis_index("fsdp")
+        self.core = lax.rem(self.dp, 2)
+        self.xy = self.dp // 2
+        self.xy_x = self.xy + 1 - 2 * lax.rem(self.xy, 2)
+        self.xy_y = lax.rem(self.xy + 2, 4)
+        self.xy_d = 3 - self.xy
+        self.sib = self.dp + 1 - 2 * self.core
+        self.dp_x = 2 * self.xy_x + self.core
+        self.dp_y = 2 * self.xy_y + self.core
+        self.dp_d = 2 * self.xy_d + self.core
+        self.zs = [lax.rem(self.z + step, 4) for step in (1, 2, 3)]
+        self.to_sib = {"dp": self.sib}
+        self.to_x = {"dp": self.dp_x}
+        self.to_y = {"dp": self.dp_y}
+        self.to_z = [{"fsdp": other} for other in self.zs]
+
+    def barrier(self):
+        semaphore = pltpu.get_barrier_semaphore()
+        for device in [self.to_sib, self.to_x, self.to_y] + self.to_z:
+            pl.semaphore_signal(semaphore, inc=1, device_id=device, device_id_type=MESH_ID)
+        pl.semaphore_wait(semaphore, 6)
+
+
+class Gather:
+    def __init__(self, place, shards, whole, parts, sems):
+        self.place, self.shards, self.whole, self.parts = place, shards, whole, parts
+        (self.z_send, self.z_recv, self.send, self.recv) = sems
+        self.stages = GATHER_STAGES
+
+    @staticmethod
+    def scratch():
+        count = len(GATHER_STAGES)
+        dma = pltpu.SemaphoreType.DMA
+        return [dma((count, 3)), dma((count, 3)), dma((count, 9)), dma((count, 9))]
+
+    def z_copy(self, s, k):
+        array, first, width = self.stages[s]
+        place = self.place
+        columns = pl.ds(first, width)
+        if array == 3:
+            rows = pl.ds(pl.multiple_of(384 * place.dp + 96 * place.z, 96), 96)
+            target = self.whole[3].at[rows, columns]
+        else:
+            target = self.parts[array].at[k, :, columns]
+        return remote(
+            self.shards[array].at[:, columns],
+            target,
+            self.z_send.at[s, k],
+            self.z_recv.at[s, k],
+            place.to_z[k],
+        )
+
+    def block(self, s, dp, half=None):
+        array, first, width = self.stages[s]
+        count = 4 * SHARE_ROWS[array]
+        start = count * dp
+        if half is not None:
+            count = count // 2
+            start = start + half * count
+        return self.whole[array].at[
+            pl.ds(pl.multiple_of(start, 48), count), pl.ds(first, width)
+        ]
+
+    def hop(self, s, index):
+        place = self.place
+        dp, half, device = (
+            (place.dp, None, place.to_x),
+            (place.dp, None, place.to_y),
+            (place.dp_x, 0, place.to_y),
+            (place.dp_y, 1, place.to_x),
+            (place.dp, None, place.to_sib),
+            (place.dp_x, None, place.to_sib),
+            (place.dp_y, None, place.to_sib),
+            (place.dp_d, 0, place.to_sib),
+            (place.dp_d, 1, place.to_sib),
+        )[index]
+        block = self.block(s, dp, half)
+        return remote(block, block, self.send.at[s, index], self.recv.at[s, index], device)
+
+    def begin(self, s):
+        for k in range(3):
+            self.z_copy(s, k).start()
+
+    def spread(self, s):
+        array, first, width = self.stages[s]
+        place = self.place
+        columns = pl.ds(first, width)
+        for k in range(3):
+            self.z_copy(s, k).wait_recv()
+        if array == 3:
+            rows = pl.ds(pl.multiple_of(384 * place.dp + 96 * place.z, 96), 96)
+            self.whole[3][rows, columns] = self.shards[3][:, columns]
+        else:
+            pieces = []
+            for other in range(4):
+                piece = self.shards[array][:, columns]
+                for k in range(3):
+                    here = lax.rem(place.z + 3 - k, 4) == other
+                    piece = jnp.where(here, self.parts[array][k, :, columns], piece)
+                pieces.append(piece)
+            rows = pl.ds(pl.multiple_of(96 * place.dp, 96), 96)
+            self.whole[array][rows, columns] = jnp.concatenate(pieces, axis=0)
+        for index in (0, 1, 4):
+            self.hop(s, index).start()
+
+    def relay(self, s):
+        self.hop(s, 0).wait_recv()
+        self.hop(s, 2).start()
+        self.hop(s, 5).start()
+        self.hop(s, 1).wait_recv()
+        self.hop(s, 3).start()
+        self.hop(s, 6).start()
+
+    def hand_over(self, s):
+        self.hop(s, 2).wait_recv()
+        self.hop(s, 7).start()
+        self.hop(s, 3).wait_recv()
+        self.hop(s, 8).start()
+
+    def arrive(self, s):
+        for index in range(4, 9):
+            self.hop(s, index).wait_recv()
+
+    def step(self, t):
+        count = len(self.stages)
+        for lag, work in enumerate((self.spread, self.relay, self.hand_over, self.arrive)):
+            if 0 <= t - lag < count:
+                work(t - lag)
+
+    def finish(self):
+        for s in range(len(self.stages)):
+            for k in range(3):
+                self.z_copy(s, k).wait_send()
+            for index in range(9):
+                self.hop(s, index).wait_send()
+
+
+SCATTER_WIDTHS = (3 * D, D + PROJ, 2 * FF, 4 * D)
+SCATTER_STAGES = (
+    (3, 0, 1536),
+    (3, 1536, 1536),
+    (2, 0, 1536),
+    (2, 1536, 1536),
+    (2, 3072, 1536),
+    (2, 4608, 1536),
+    (1, 0, 896),
+    (0, 0, 768),
+    (0, 768, 768),
+    (0, 1536, 768),
+)
+SCATTER_SLOTS = (
+    (0, 0, None),
+    (1, 0, None),
+    (2, 0, None),
+    (3, 0, None),
+    (0, 0, 0),
+    (1, 0, 1),
+    (2, 0, 2),
+    (3, 0, 3),
+    (3, 768, 3),
+    (0, 0, 4),
+)
+
+
+class Scatter:
+    def __init__(self, place, buffers, settled, sems):
+        self.place, self.settled = place, settled
+        self.local_all, self.sib_all = buffers[0:2]
+        self.from_x, self.from_y = buffers[2:6], buffers[6:10]
+        self.diag_x, self.diag_y = buffers[10:14], buffers[14:18]
+        self.z_out, self.z_in = buffers[18:22], buffers[22:26]
+        self.send, self.recv, self.credit = sems
+        self.begun = {}
+        self.sent = set()
+
+    @staticmethod
+    def scratch():
+        kind = jnp.bfloat16
+        shapes = [pltpu.VMEM((4, 4, 2, 96, 1536), kind), pltpu.VMEM((4, 4, 96, 1536), kind)]
+        shapes += [pltpu.VMEM((96, w), kind) for w in SCATTER_WIDTHS] * 2
+        shapes += [pltpu.VMEM((48, w), kind) for w in SCATTER_WIDTHS] * 2
+        pieces = [(24, w) for w in SCATTER_WIDTHS[:3]] + [(96, D)]
+        shapes += [pltpu.VMEM((4, r, w), kind) for r, w in pieces]
+        shapes += [pltpu.VMEM((3, r, w), kind) for r, w in pieces]
+        return shapes
+
+    @staticmethod
+    def semaphores():
+        count = len(SCATTER_STAGES)
+        dma = pltpu.SemaphoreType.DMA
+        return [dma((count, 8)), dma((count, 8)), pltpu.SemaphoreType.REGULAR((count,))]
+
+    def local(self, s):
+        slot, offset, _ = SCATTER_SLOTS[s]
+        width = SCATTER_STAGES[s][2]
+        return self.local_all.at[slot, :, :, :, pl.ds(offset, width)]
+
+    def columns(self, s):
+        return pl.ds(SCATTER_STAGES[s][1], SCATTER_STAGES[s][2])
+
+    def z_columns(self, s):
+        array, first, width = SCATTER_STAGES[s]
+        return pl.ds(first // 4, width // 4) if array == 3 else pl.ds(first, width)
+
+    def copy(self, s, index):
+        array, first, width = SCATTER_STAGES[s]
+        place = self.place
+        columns = self.columns(s)
+        local = self.local(s)
+        if index == 0:
+            source = local.at[:, 1 - place.core]
+            target = self.sib_all.at[s % 4, :, :, pl.ds(0, width)]
+            device = place.to_sib
+        elif index == 1:
+            source = local.at[place.xy_d, place.core, pl.ds(0, 48)]
+            target = self.diag_x[array].at[:, columns]
+            device = place.to_x
+        elif index == 2:
+            source = local.at[place.xy_d, place.core, pl.ds(48, 48)]
+            target = self.diag_y[array].at[:, columns]
+            device = place.to_y
+        elif index == 3:
+            source = local.at[place.xy_x, place.core]
+            target = self.from_x[array].at[:, columns]
+            device = place.to_x
+        elif index == 4:
+            source = local.at[place.xy_y, place.core]
+            target = self.from_y[array].at[:, columns]
+            device = place.to_y
+        else:
+            k = index - 5
+            source = self.z_out[array].at[place.zs[k], :, self.z_columns(s)]
+            target = self.z_in[array].at[k, :, self.z_columns(s)]
+            device = place.to_z[k]
+        return remote(source, target, self.send.at[s, index], self.recv.at[s, index], device)
+
+    def add(self, s, block, other, rows=slice(None)):
+        local = self.local(s)
+        here = (block, self.place.core, rows)
+        total = local[here].astype(jnp.float32) + other.astype(jnp.float32)
+        local[here] = total.astype(jnp.bfloat16)
+
+    def free(self, s):
+        before = SCATTER_SLOTS[s][2]
+        if before is not None and before not in self.sent:
+            self.sent.add(before)
+            for index in range(5):
+                self.copy(before, index).wait_send()
+
+    def begin(self, s):
+        if s >= 4:
+            pl.semaphore_wait(self.credit.at[s], 1)
+        self.copy(s, 0).start()
+
+    def pair(self, s):
+        place = self.place
+        columns = pl.ds(0, SCATTER_STAGES[s][2])
+        self.copy(s, 0).wait_recv()
+        self.add(s, place.xy_d, self.sib_all[s % 4, place.xy_d, :, columns])
+        self.copy(s, 1).start()
+        self.copy(s, 2).start()
+        for block in (place.xy_x, place.xy_y, place.xy):
+            self.add(s, block, self.sib_all[s % 4, block, :, columns])
+        if s + 4 < len(SCATTER_STAGES):
+            pl.semaphore_signal(
+                self.credit.at[s + 4], inc=1, device_id=place.to_sib, device_id_type=MESH_ID
+            )
+
+    def cross(self, s):
+        array = SCATTER_STAGES[s][0]
+        place = self.place
+        columns = self.columns(s)
+        self.copy(s, 1).wait_recv()
+        self.add(s, place.xy_y, self.diag_x[array][:, columns], slice(0, 48))
+        self.copy(s, 4).start()
+        self.copy(s, 2).wait_recv()
+        self.add(s, place.xy_x, self.diag_y[array][:, columns], slice(48, 96))
+        self.copy(s, 3).start()
+
+    def square(self, s):
+        array, first, width = SCATTER_STAGES[s]
+        place = self.place
+        self.copy(s, 3).wait_recv()
+        self.copy(s, 4).wait_recv()
+        local = self.local(s)
+        for other in range(4):
+            if array == 3:
+                rows, inside = slice(0, 96), pl.ds(384 * other, 384)
+                outside = pl.ds(first + 384 * other, 384)
+            else:
+                rows, inside = slice(24 * other, 24 * other + 24), pl.ds(0, width)
+                outside = pl.ds(first, width)
+            total = (
+                local[place.xy, place.core, rows, inside].astype(jnp.float32)
+                + self.from_x[array][rows, outside].astype(jnp.float32)
+                + self.from_y[array][rows, outside].astype(jnp.float32)
+            )
+            self.z_out[array][other, :, self.z_columns(s)] = total.astype(jnp.bfloat16)
+        for k in range(3):
+            self.copy(s, 5 + k).start()
+
+    def settle(self, s):
+        array = SCATTER_STAGES[s][0]
+        columns = self.z_columns(s)
+        total = self.z_out[array][self.place.z, :, columns].astype(jnp.float32)
+        for k in range(3):
+            self.copy(s, 5 + k).wait_recv()
+            total = total + self.z_in[array][k, :, columns].astype(jnp.float32)
+        self.settled(s, total)
+
+    def step(self, turn, s=None):
+        if s is not None:
+            self.begun[s] = turn
+        for other in sorted(self.begun, reverse=True):
+            lag = turn - self.begun[other]
+            if lag < 5:
+                (self.begin, self.pair, self.cross, self.square, self.settle)[lag](other)
+
+    def finish(self):
+        for s in range(len(SCATTER_STAGES)):
+            for index in range(8):
+                if index >= 5 or s not in self.sent:
+                    self.copy(s, index).wait_send()
+
+
+ROW_BLOCK = 128
+SCALE = 0.7978845608028654
+BF = jnp.bfloat16
+F32 = jnp.float32
+ROWS_ALL = 768
+NEAR = 3 * ROW_BLOCK
+
+
+def dot(left, right, left_dim=1, right_dim=0):
+    return lax.dot_general(
+        left, right, (((left_dim,), (right_dim,)), ((), ())), preferred_element_type=F32
+    )
+
+
+def loop(count, body):
+    def step(index, carry):
+        body(index)
+        return carry
+
+    lax.fori_loop(0, count, step, 0)
+
+
+def aligned(start, multiple, size):
+    return pl.ds(pl.multiple_of(start, multiple), size)
+
+
+def unflatten(flat, wide, target, start_of):
+    lines = flat.shape[0]
+    rows = target.shape[0]
+    blocks = lines // rows
+    wide[0:lines] = flat[...].astype(F32)
+    for block in range(blocks):
+        first = start_of(block)
+        target[:, first : first + 128] = wide[pl.ds(block, rows, blocks), :].astype(BF)
+
+
+def marks_of(relative):
+    distance = jnp.abs(relative)
+    distant = jnp.full_like(distance, 8)
+    for power in range(1, 8):
+        distant = distant + (distance * distance >= 64 * 2**power).astype(jnp.int32)
+    bucket = jnp.where(distance < 8, distance, distant)
+    bucket = bucket + 16 * (relative > 0).astype(jnp.int32)
+    labels = lax.broadcasted_iota(jnp.int32, relative.shape, 0)
+    return bucket == labels
+
+
+def normed(values, gain_row):
+    inverse = lax.rsqrt(jnp.mean(values * values, axis=-1, keepdims=True) + EPSILON)
+    return values * inverse * gain_row
+
+
+def window(block):
+    return max(0, block - 2), min(3, block + 2)
+
+
+def head_lanes(rows, which):
+    lane = lax.broadcasted_iota(jnp.int32, (rows, 128), 1)
+    return lane < HEAD_DIM if which == 0 else lane >= HEAD_DIM
+
+
+def keep(values, which):
+    return jnp.where(head_lanes(values.shape[0], which), values, jnp.zeros_like(values))
+
+
+def softmax_rows(scores):
+    largest = jnp.max(scores, axis=-1, keepdims=True)
+    powers = jnp.exp(scores - largest)
+    return (powers * (1.0 / jnp.sum(powers, axis=-1, keepdims=True))).astype(BF)
+
+
+FORWARD_SAVED = (
+    ((768, 3 * D), BF),
+    ((768, D + PROJ), BF),
+    ((768, 2 * FF), BF),
+    ((FF, D), BF),
+    ((768, D), BF),
+    ((768, 3 * D), BF),
+    ((768, D), BF),
+    ((768, D), F32),
+    ((768, D), BF),
+    ((768, 2 * FF), BF),
+    ((768, FF), BF),
+    ((768, D), F32),
+    ((768, D), BF),
+    ((6, 512, 1024), BF),
+    ((256, 1536), BF),
+)
+
+
+def forward_kernel(*refs):
+    (doc, qry, doc_lengths, qry_lengths, small) = refs[0:5]
+    flats = refs[5:13]
+    doc_out, qry_out, gains_out = refs[13:16]
+    saved = refs[16:31]
+    rest = refs[31:]
+    whole, parts, shards = rest[0:4], rest[4:7], rest[7:11]
+    (wide, small_in, gains, diagonals, bias, id_column, id_row) = rest[11:18]
+    (norm_one, qkv, context, hidden, norm_two, factors, inner, norm_three) = rest[18:26]
+    (prob_doc, prob_qry, scores) = rest[26:29]
+    gather_sems = rest[29:33]
+    small_send, small_recv, save_sem, whole_sem = rest[33:37]
+
+    place = Place()
+    place.barrier()
+    gains[...] = jnp.zeros_like(gains)
+    gather = Gather(place, shards, whole, parts, gather_sems)
+
+    def small_copy(k):
+        return remote(
+            small, small_in.at[k], small_send.at[k], small_recv.at[k], place.to_z[k]
+        )
+
+    for k in range(3):
+        small_copy(k).start()
+    for index in range(3):
+        unflatten(flats[index], wide, shards[0].at[:, D * index : D * index + D], lambda j: 128 * j)
+        gather.begin(index)
+    unflatten(flats[3], wide, shards[1].at[:, 0:D], lambda j: 128 * j)
+    shards[1][:, D:] = flats[7][...]
+    gather.begin(3)
+    unflatten(flats[4], wide, shards[2], lambda j: 1536 * (j // 6) + 128 * (j % 6))
+    unflatten(flats[5], wide, shards[2], lambda j: 1536 * (j // 6) + 128 * (j % 6) + D)
+    for index in range(4, 8):
+        gather.begin(index)
+    unflatten(flats[6], wide, shards[3], lambda j: 128 * j)
+    for index in range(8, 10):
+        gather.begin(index)
+
+    saves = []
+
+    def save(index, source, target=None):
+        copy = pltpu.make_async_copy(
+            source, saved[index] if target is None else target, save_sem.at[index]
+        )
+        copy.start()
+        saves.append((index, copy))
+        return copy
+
+    def save_whole(s):
+        array, first, width = GATHER_STAGES[s]
+        columns = pl.ds(first, width)
+        copy = pltpu.make_async_copy(
+            whole[array].at[:, columns], saved[array].at[:, columns], whole_sem.at[s]
+        )
+        copy.start()
+        saves.append((-1, copy))
+
+    def small_arrive():
+        for k in range(3):
+            small_copy(k).wait_recv()
+        pieces = []
+        for other in range(4):
+            piece = small[...]
+            for k in range(3):
+                here = lax.rem(place.z + 3 - k, 4) == other
+                piece = jnp.where(here, small_in[k], piece)
+            pieces.append(piece)
+        low = lax.broadcasted_iota(jnp.int32, (1, 128), 1) < 64
+        for row in range(3):
+            for tile in range(6):
+                unit = 12 * row + 2 * tile
+                left = pieces[unit // 9][unit % 9 : unit % 9 + 1, :]
+                unit = unit + 1
+                right = pieces[unit // 9][unit % 9 : unit % 9 + 1, :]
+                gains[row : row + 1, 128 * tile : 128 * tile + 128] = jnp.where(low, left, right)
+        gains_out[...] = gains[...]
+        table = jnp.concatenate([piece[16:24, :] for piece in pieces], axis=0).astype(BF)
+        relative = lax.broadcasted_iota(jnp.int32, (BUCKETS, 512), 1) - 256
+        diagonals[...] = dot(table, marks_of(relative).astype(BF), 0, 0)[0:16]
+
+    def make_bias(head):
+        rows = jnp.broadcast_to(diagonals[pl.ds(head, 1), :], (8, 512))
+        lines = lax.broadcasted_iota(jnp.int32, (8, 512), 0)
+        for bit in range(3):
+            moved = pltpu.roll(rows, 2**bit, 1)
+            rows = jnp.where(lax.rem(lines // 2**bit, 2) == 1, moved, rows)
+        for group in range(ROW_BLOCK // 8):
+            moved = pltpu.roll(rows, 8 * group, 1) if group else rows
+            bias[head, 8 * group : 8 * group + 8, :] = moved[:, 128:512]
+
+    def make_ids():
+        position = lax.broadcasted_iota(jnp.int32, (512, 128), 0)
+        across = lax.broadcasted_iota(jnp.int32, (8, 512), 1)
+        down_id, across_id = jnp.zeros_like(position), jnp.zeros_like(across)
+        edge = 0
+        for index in range(4):
+            edge = edge + doc_lengths[0, index]
+            down_id = down_id + (position >= edge).astype(jnp.int32)
+            across_id = across_id + (across >= edge).astype(jnp.int32)
+        id_column[0:512] = down_id
+        id_row[:, 0:512] = across_id
+        position = lax.broadcasted_iota(jnp.int32, (32, 128), 0)
+        across = lax.broadcasted_iota(jnp.int32, (8, 256), 1)
+        across_id = jnp.zeros_like(across)
+        for index in range(8):
+            length = qry_lengths[0, index]
+            id_column[512 + 32 * index : 544 + 32 * index] = 2 * index + (
+                position >= length
+            ).astype(jnp.int32)
+            mine = (across >= 32 * index) & (across < 32 * index + 32)
+            value = 2 * index + (across >= length + 32 * index).astype(jnp.int32)
+            across_id = jnp.where(mine, value, across_id)
+        id_row[:, 512:768] = across_id
+
+    def first_norm():
+        gain = gains[0:1, :]
+
+        def documents(index):
+            rows = aligned(128 * index, 128, 128)
+            norm_one[rows] = normed(doc[rows].astype(F32), gain).astype(BF)
+
+        def queries(index):
+            rows = aligned(128 * index, 128, 128)
+            norm_one[aligned(512 + 128 * index, 128, 128)] = normed(
+                qry[rows].astype(F32), gain
+            ).astype(BF)
+
+        loop(4, documents)
+        loop(2, queries)
+        save(4, norm_one)
+
+    def project(index):
+        columns = pl.ds(D * index, D)
+        qkv[:, columns] = dot(norm_one[...], whole[0][:, columns]).astype(BF)
+
+    def attend_pair(pair):
+        query = qkv[0:512, aligned(128 * pair, 128, 128)]
+        key = qkv[0:512, aligned(D + 128 * pair, 128, 128)]
+        value = qkv[0:512, aligned(2 * D + 128 * pair, 128, 128)]
+        for which in range(2):
+            head = 2 * pair + which
+            scores[...] = dot(keep(query, which), key, 1, 1)
+            far_left = jnp.broadcast_to(bias[head, 127:128, 0:1], (128, 128))
+            far_right = jnp.broadcast_to(bias[head, 0:1, NEAR - 1 : NEAR], (128, 128))
+            for block in range(4):
+                low, high = window(block)
+                near_low, near_high = max(low, block - 1), min(high, block + 1)
+                pieces = [far_left] * (near_low - low)
+                pieces.append(
+                    bias[
+                        head,
+                        :,
+                        128 * (near_low - block + 1) : 128 * (near_high - block + 2),
+                    ]
+                )
+                pieces += [far_right] * (high - near_high)
+                rows = slice(128 * block, 128 * block + 128)
+                columns = slice(128 * low, 128 * high + 128)
+                allowed = id_column[rows, 0:1] == id_row[0:1, columns]
+                values = scores[rows, columns] + jnp.concatenate(pieces, axis=1)
+                share = softmax_rows(jnp.where(allowed, values, NEGATIVE))
+                prob_doc[
+                    pair, rows, 512 * which + 128 * low : 512 * which + 128 * high + 128
+                ] = share
+        both = jnp.concatenate([keep(value, 0), keep(value, 1)], axis=0)
+        context[0:512, aligned(128 * pair, 128, 128)] = dot(prob_doc[pair], both).astype(BF)
+        for block in range(2):
+            rows = slice(512 + 128 * block, 640 + 128 * block)
+            query = qkv[rows, aligned(128 * pair, 128, 128)]
+            key = qkv[rows, aligned(D + 128 * pair, 128, 128)]
+            value = qkv[rows, aligned(2 * D + 128 * pair, 128, 128)]
+            allowed = id_column[rows, 0:1] == id_row[0:1, rows]
+            shares = []
+            for which in range(2):
+                values = dot(keep(query, which), key, 1, 1)
+                values = values + bias[2 * pair + which, :, 128:256]
+                shares.append(softmax_rows(jnp.where(allowed, values, NEGATIVE)))
+            shares = jnp.concatenate(shares, axis=1)
+            prob_qry[128 * block : 128 * block + 128, aligned(256 * pair, 128, 256)] = shares
+            both = jnp.concatenate([keep(value, 0), keep(value, 1)], axis=0)
+            context[rows, aligned(128 * pair, 128, 128)] = dot(shares, both).astype(BF)
+
+    def attend(first, last):
+        lax.fori_loop(first, last, lambda pair, carry: (attend_pair(pair), carry)[1], 0)
+
+    def after_attention():
+        save(5, qkv)
+        save(6, context)
+        save(13, prob_doc)
+        save(14, prob_qry)
+
+        def one(tokens, offset):
+            def block(index):
+                source = aligned(128 * index, 128, 128)
+                rows = aligned(offset + 128 * index, 128, 128)
+                total = tokens[source].astype(F32) + dot(context[rows], whole[1][:, 0:D])
+                hidden[rows] = total
+                norm_two[rows] = normed(total, gains[1:2, :]).astype(BF)
+
+            return block
+
+        loop(4, one(doc, 0))
+        loop(2, one(qry, 512))
+        copy = save(7, hidden)
+        save(8, norm_two)
+        return copy
+
+    def gated(chunk):
+        def block(index):
+            rows = aligned(256 * index, 256, 256)
+            left = norm_two[rows]
+            gate = dot(left, whole[2][:, 1536 * chunk : 1536 * chunk + D])
+            upper = dot(left, whole[2][:, 1536 * chunk + D : 1536 * chunk + 2 * D])
+            square = gate * gate
+            bend = jnp.tanh(SCALE * gate * (1.0 + 0.044715 * square))
+            half = 0.5 * (1.0 + bend)
+            active = gate * half
+            slope = half + 0.5 * gate * (1.0 - bend * bend) * (
+                SCALE + (3.0 * 0.044715 * SCALE) * square
+            )
+            inner[rows, D * chunk : D * chunk + D] = (active * upper).astype(BF)
+            factors[rows, 1536 * chunk : 1536 * chunk + D] = (upper * slope).astype(BF)
+            factors[rows, 1536 * chunk + D : 1536 * chunk + 2 * D] = active.astype(BF)
+
+        loop(3, block)
+
+    def descend(half):
+        columns = slice(384 * half, 384 * half + 384)
+
+        def block(index):
+            rows = aligned(256 * index, 256, 256)
+            hidden[rows, columns] = hidden[rows, columns] + dot(inner[rows], whole[3][:, columns])
+
+        loop(3, block)
+
+    def last():
+        def block(index):
+            rows = aligned(128 * index, 128, 128)
+            norm_three[rows] = normed(hidden[rows], gains[2:3, :]).astype(BF)
+
+        loop(6, block)
+        result = dot(norm_three[...], whole[1][:, D:]).astype(BF)
+        doc_out[...] = result[0:512]
+        qry_out[...] = result[512:768]
+        save(11, hidden)
+        save(12, norm_three)
+
+    def clear(pair):
+        nothing = jnp.zeros((128, 128), BF)
+        for which in range(2):
+            prob_doc[pair, 0:128, 512 * which + 384 : 512 * which + 512] = nothing
+            prob_doc[pair, 384:512, 512 * which : 512 * which + 128] = nothing
+
+    count = len(GATHER_STAGES)
+    hidden_copy = None
+    for t in range(count + 3):
+        gather.step(t)
+        if t >= 3:
+            save_whole(t - 3)
+        if t == 0:
+            small_arrive()
+            loop(12, make_bias)
+            make_ids()
+            loop(6, clear)
+        if t == 1:
+            first_norm()
+        if 3 <= t < 6:
+            project(t - 3)
+        if t == 5:
+            attend(0, 1)
+        if t == 6:
+            attend(1, 4)
+        if t == 7:
+            attend(4, 6)
+            hidden_copy = after_attention()
+        if 8 <= t < 12:
+            gated(t - 8)
+        if t == 11:
+            save(9, factors)
+            save(10, inner)
+            hidden_copy.wait()
+            descend(0)
+        if t == 12:
+            descend(1)
+    last()
+    gather.finish()
+    for k in range(3):
+        small_copy(k).wait_send()
+    for index, copy in saves:
+        if index != 7:
+            copy.wait()
+
+
+def forward(doc, qry, doc_lengths, qry_lengths, small, flats):
+    vmem = pl.BlockSpec(memory_space=pltpu.VMEM)
+    smem = pl.BlockSpec(memory_space=pltpu.SMEM)
+    hbm = pl.BlockSpec(memory_space=pl.ANY)
+    dma = pltpu.SemaphoreType.DMA
+    whole_rows = [32 * count for count in SHARE_ROWS]
+    scratch = [pltpu.VMEM((r, w), BF) for r, w in zip(whole_rows, WIDTHS)]
+    scratch += [pltpu.VMEM((3, r, w), BF) for r, w in zip(SHARE_ROWS[:3], WIDTHS[:3])]
+    scratch += [pltpu.VMEM((r, w), BF) for r, w in zip(SHARE_ROWS, WIDTHS)]
+    scratch += [
+        pltpu.VMEM((576, 128), F32),
+        pltpu.VMEM((3, 24, 128), F32),
+        pltpu.VMEM((8, D), F32),
+        pltpu.VMEM((16, 512), F32),
+        pltpu.VMEM((HEADS, 128, NEAR), F32),
+        pltpu.VMEM((768, 128), jnp.int32),
+        pltpu.VMEM((8, 768), jnp.int32),
+        pltpu.VMEM((768, D), BF),
+        pltpu.VMEM((768, 3 * D), BF),
+        pltpu.VMEM((768, D), BF),
+        pltpu.VMEM((768, D), F32),
+        pltpu.VMEM((768, D), BF),
+        pltpu.VMEM((768, 2 * FF), BF),
+        pltpu.VMEM((768, FF), BF),
+        pltpu.VMEM((768, D), BF),
+        pltpu.VMEM((6, 512, 1024), BF),
+        pltpu.VMEM((256, 1536), BF),
+        pltpu.VMEM((512, 512), F32),
+    ]
+    scratch += Gather.scratch()
+    scratch += [dma((3,)), dma((3,)), dma((15,)), dma((len(GATHER_STAGES),))]
+    return pl.pallas_call(
+        forward_kernel,
+        out_shape=(
+            jax.ShapeDtypeStruct((512, PROJ), BF),
+            jax.ShapeDtypeStruct((256, PROJ), BF),
+            jax.ShapeDtypeStruct((8, D), F32),
+        )
+        + tuple(jax.ShapeDtypeStruct(shape, kind) for shape, kind in FORWARD_SAVED),
+        in_specs=[vmem, vmem, smem, smem, vmem] + [vmem] * 8,
+        out_specs=(vmem, vmem, vmem) + (hbm,) * len(FORWARD_SAVED),
+        scratch_shapes=scratch,
+        compiler_params=pltpu.CompilerParams(
+            collective_id=0, has_side_effects=True, vmem_limit_bytes=VMEM_LIMIT
+        ),
+        name="forward",
+    )(doc, qry, doc_lengths, qry_lengths, small, *flats)
+
+
+VMEM_LIMIT = 63 * 2**20
+
+
+def norm_back(values, gain_row, incoming):
+    inverse = lax.rsqrt(jnp.mean(values * values, axis=-1, keepdims=True) + EPSILON)
+    scaled = gain_row * incoming
+    inner = jnp.mean(scaled * values, axis=-1, keepdims=True)
+    result = inverse * scaled - values * (inverse * inverse * inverse * inner)
+    terms = incoming * values * inverse
+    return result, jnp.sum(terms.reshape(-1, 8, D), axis=0)
+
+
+def diagonal_sums(near):
+    wide = jnp.concatenate([near, jnp.zeros((128, 128), F32)], axis=1)
+    rows = wide[0:8]
+    for group in range(1, 16):
+        rows = rows + pltpu.roll(wide[8 * group : 8 * group + 8], 512 - 8 * group, 1)
+    lines = lax.broadcasted_iota(jnp.int32, (8, 512), 0)
+    for bit in range(3):
+        moved = pltpu.roll(rows, 512 - 2**bit, 1)
+        rows = jnp.where(lax.rem(lines // 2**bit, 2) == 1, moved, rows)
+    return jnp.sum(rows, axis=0, keepdims=True)
+
+
+def backward_kernel(*refs):
+    doc, qry, doc_cotangent, qry_cotangent, gains = refs[0:5]
+    saved = refs[5:20]
+    doc_grad, qry_grad = refs[20:22]
+    flats = refs[22:30]
+    small_out = refs[30]
+    rest = refs[31:]
+    (out_mat, down, gate_up, factors, mixed, residual, hidden, incoming) = rest[0:8]
+    (norm_two, norm_three, narrow, context, cotangent) = rest[8:13]
+    (gain_terms, diagonal_rows, scores, small, small_in) = rest[13:18]
+    scatter_buffers = rest[18:44]
+    scatter_sems = rest[44:47]
+    small_send, small_recv, load_sem = rest[47:50]
+
+    place = Place()
+    loads = {}
+
+    def load(name, source, target):
+        copy = pltpu.make_async_copy(source, target, load_sem.at[len(loads)])
+        copy.start()
+        loads[name] = copy
+
+    def ready(*names):
+        for name in names:
+            loads[name].wait()
+
+    load("residual", saved[11], residual)
+    load("out_mat", saved[1], out_mat)
+    load("inner", saved[10], mixed)
+    load("down", saved[3], down)
+
+    def load_chunk(chunk):
+        columns = pl.ds(1536 * chunk, 1536)
+        load(("factors", chunk), saved[9].at[:, columns], factors.at[chunk % 2])
+        load(("gate_up", chunk), saved[2].at[:, columns], gate_up.at[chunk % 2])
+
+    load_chunk(0)
+    load("norm_two", saved[8], norm_two)
+    load_chunk(1)
+    load("hidden", saved[7], hidden)
+    load("context", saved[6], context)
+    load("norm_three", saved[12], norm_three)
+
+    place.barrier()
+
+    def settled(s, total):
+        array, first, width = SCATTER_STAGES[s]
+        if array == 3:
+            for tile in range(3):
+                line = 3 * (first // 1536) + tile
+                flats[6][pl.ds(line, 96, 6), :] = total[:, 128 * tile : 128 * tile + 128]
+        elif array == 2:
+            for tile in range(12):
+                line = 6 * (first // 1536) + tile % 6
+                flats[4 + tile // 6][pl.ds(line, 24, 24), :] = total[
+                    :, 128 * tile : 128 * tile + 128
+                ]
+        else:
+            for tile in range(6):
+                flats[3 if array == 1 else first // D][pl.ds(tile, 24, 6), :] = total[
+                    :, 128 * tile : 128 * tile + 128
+                ]
+            if array == 1:
+                flats[7][...] = total[:, D:]
+
+    scatter = Scatter(place, scatter_buffers, settled, scatter_sems)
+    gain_terms[...] = jnp.zeros_like(gain_terms)
+    diagonal_rows[...] = jnp.zeros_like(diagonal_rows)
+    cotangent[0:512] = doc_cotangent[...]
+    cotangent[512:768] = qry_cotangent[...]
+
+    def final_norm(index):
+        rows = aligned(128 * index, 128, 128)
+        grad, terms = norm_back(
+            residual[rows], gains[2:3, :], dot(cotangent[rows], out_mat[:, D:], 1, 1)
+        )
+        residual[rows] = grad
+        narrow[rows] = grad.astype(BF)
+        gain_terms[2] = gain_terms[2] + terms
+
+    ready("residual", "out_mat")
+    loop(6, final_norm)
+
+    ready("inner")
+    for half in range(2):
+        scatter.free(half)
+        local = scatter.local(half)
+
+        def piece(index):
+            total = dot(
+                mixed[:, aligned(D * index, 128, D)],
+                narrow[:, 384 * half : 384 * half + 384],
+                0,
+                0,
+            ).astype(BF)
+            for core in range(2):
+                for other in range(4):
+                    first = 384 * core + 96 * other
+                    local[index, core, :, 384 * other : 384 * other + 384] = total[
+                        first : first + 96
+                    ]
+
+        loop(4, piece)
+        scatter.step(half, half)
+    load("qkv", saved[5], mixed.at[:, pl.ds(0, 3 * D)])
+    load("norm_one", saved[4], mixed.at[:, pl.ds(3 * D, D)])
+
+    def put(local, total, first):
+        total = total.astype(BF)
+        width = total.shape[1]
+        for block in range(8):
+            local[block // 2, block % 2, :, first : first + width] = total[
+                96 * block : 96 * block + 96
+            ]
+
+    ready("down", "norm_two")
+    for chunk in range(4):
+        slot = chunk % 2
+        ready(("factors", chunk), ("gate_up", chunk))
+
+        def gated_back(index):
+            rows = aligned(256 * index, 256, 256)
+            grad = dot(narrow[rows], down[D * chunk : D * chunk + D], 1, 1)
+            for side in (0, D):
+                factors[slot, rows, side : side + D] = (
+                    grad * factors[slot, rows, side : side + D].astype(F32)
+                ).astype(BF)
+
+        loop(3, gated_back)
+        stage = 2 + chunk
+        scatter.free(stage)
+        for side in (0, D):
+            put(
+                scatter.local(stage),
+                dot(norm_two[...], factors[slot, :, side : side + D], 0, 0),
+                side,
+            )
+        scatter.step(stage, stage)
+
+        def collect(index):
+            rows = aligned(256 * index, 256, 256)
+            part = dot(factors[slot, rows], gate_up[slot], 1, 1)
+            incoming[rows] = part if chunk == 0 else incoming[rows] + part
+
+        loop(3, collect)
+        if chunk < 2:
+            load_chunk(chunk + 2)
+        if chunk == 2:
+            load(("share", 0), saved[13].at[0], factors.at[0, pl.ds(0, 512), pl.ds(0, 1024)])
+            load("share_qry", saved[14], gate_up.at[0, pl.ds(0, 256)])
+    load(("share", 1), saved[13].at[1], factors.at[1, pl.ds(0, 512), pl.ds(0, 1024)])
+    for index in range(3):
+        load(
+            ("qkv_mat", index),
+            saved[0].at[:, pl.ds(D * index, D)],
+            down.at[pl.ds(D * index, D)],
+        )
+    load("doc", doc, down.at[pl.ds(3 * D, 512)])
+    load("qry", qry, down.at[pl.ds(3 * D + 512, 256)])
+
+    def middle_norm(index):
+        rows = aligned(128 * index, 128, 128)
+        grad, terms = norm_back(hidden[rows], gains[1:2, :], incoming[rows])
+        grad = grad + residual[rows]
+        residual[rows] = grad
+        narrow[rows] = grad.astype(BF)
+        gain_terms[1] = gain_terms[1] + terms
+
+    ready("hidden")
+    loop(6, middle_norm)
+    ready("context", "norm_three")
+    scatter.free(6)
+    put(scatter.local(6), dot(context[...], narrow[...], 0, 0), 0)
+    put(scatter.local(6), dot(norm_three[...], cotangent[...], 0, 0), D)
+    scatter.step(6, 6)
+    grad_context = norm_three
+    grad_context[...] = dot(narrow[...], out_mat[:, 0:D], 1, 1).astype(BF)
+
+    nothing = jnp.zeros((128, 128), BF)
+    grad_scores = gate_up.at[1]
+    for which in range(2):
+        grad_scores[0:128, 512 * which + 384 : 512 * which + 512] = nothing
+        grad_scores[384:512, 512 * which : 512 * which + 128] = nothing
+
+    def two(values):
+        return jnp.concatenate([keep(values, 0), keep(values, 1)], axis=0)
+
+    def attention_back(pair, share):
+        columns = [aligned(D * index + 128 * pair, 128, 128) for index in range(3)]
+        rows = slice(0, 512)
+        query, key, value = (mixed[rows, column] for column in columns)
+        grad = grad_context[rows, columns[0]]
+        near_sums, far_sums = [], []
+        for which in range(2):
+            scores[...] = dot(keep(grad, which), value, 1, 1)
+            near = [None, None, None]
+            far = [None, None]
+            for block in range(4):
+                low, high = window(block)
+                rows_here = slice(128 * block, 128 * block + 128)
+                reach = slice(512 * which + 128 * low, 512 * which + 128 * high + 128)
+                part = share[rows_here, reach].astype(F32)
+                grad_share = scores[rows_here, 128 * low : 128 * high + 128]
+                weighted = jnp.sum(part * grad_share, axis=-1, keepdims=True)
+                result = (part * (grad_share - weighted)).astype(BF)
+                grad_scores[rows_here, reach] = result
+                result = result.astype(F32)
+                for other in range(low, high + 1):
+                    tile = result[:, 128 * (other - low) : 128 * (other - low) + 128]
+                    place_at = other - block
+                    if abs(place_at) == 2:
+                        side = 0 if place_at < 0 else 1
+                        far[side] = tile if far[side] is None else far[side] + tile
+                    else:
+                        side = place_at + 1
+                        near[side] = tile if near[side] is None else near[side] + tile
+            near_sums.append(near)
+            far_sums.append(far)
+        grad_query = dot(grad_scores[0:512, 0:1024], two(key))
+        grad_key = dot(grad_scores[0:512, 0:512], keep(query, 0), 0, 0) + dot(
+            grad_scores[0:512, 512:1024], keep(query, 1), 0, 0
+        )
+        grad_value = dot(share[0:512, 0:512], keep(grad, 0), 0, 0) + dot(
+            share[0:512, 512:1024], keep(grad, 1), 0, 0
+        )
+        mixed[rows, columns[0]] = grad_query.astype(BF)
+        mixed[rows, columns[1]] = grad_key.astype(BF)
+        mixed[rows, columns[2]] = grad_value.astype(BF)
+        for block in range(2):
+            rows = slice(512 + 128 * block, 640 + 128 * block)
+            query, key, value = (mixed[rows, column] for column in columns)
+            grad = grad_context[rows, columns[0]]
+            small_share = gate_up[
+                0, 128 * block : 128 * block + 128, aligned(256 * pair, 128, 256)
+            ]
+            results = []
+            grad_key = jnp.zeros((128, 128), F32)
+            grad_value = jnp.zeros((128, 128), F32)
+            for which in range(2):
+                part = small_share[:, 128 * which : 128 * which + 128]
+                grad_share = dot(keep(grad, which), value, 1, 1)
+                wide = part.astype(F32)
+                weighted = jnp.sum(wide * grad_share, axis=-1, keepdims=True)
+                result = (wide * (grad_share - weighted)).astype(BF)
+                near_sums[which][1] = near_sums[which][1] + result.astype(F32)
+                results.append(result)
+                grad_key = grad_key + dot(result, keep(query, which), 0, 0)
+                grad_value = grad_value + dot(part, keep(grad, which), 0, 0)
+            grad_query = dot(jnp.concatenate(results, axis=1), two(key))
+            mixed[rows, columns[0]] = grad_query.astype(BF)
+            mixed[rows, columns[1]] = grad_key.astype(BF)
+            mixed[rows, columns[2]] = grad_value.astype(BF)
+        lane = lax.broadcasted_iota(jnp.int32, (1, 512), 1)
+        for which in range(2):
+            row = diagonal_sums(jnp.concatenate(near_sums[which], axis=1))
+            for side, column in ((0, 28), (1, 228)):
+                total = jnp.sum(far_sums[which][side], axis=(0, 1), keepdims=True)
+                row = row + jnp.where(lane == column, total, 0.0)
+            diagonal_rows[pl.ds(2 * pair + which, 1), :] = row
+
+    ready("qkv", "norm_one", "share_qry")
+    turn = 7
+    for pair in range(6):
+        slot = pair % 2
+        ready(("share", pair))
+        attention_back(pair, factors.at[slot])
+        if pair < 4:
+            load(
+                ("share", pair + 2),
+                saved[13].at[pair + 2],
+                factors.at[slot, pl.ds(0, 512), pl.ds(0, 1024)],
+            )
+        if pair in (1, 3):
+            scatter.step(turn)
+            turn = turn + 1
+
+    for index in range(3):
+        stage = 7 + index
+        scatter.free(stage)
+        put(
+            scatter.local(stage),
+            dot(mixed[:, 3 * D :], mixed[:, D * index : D * index + D], 0, 0),
+            0,
+        )
+        scatter.step(turn, stage)
+        turn = turn + 1
+
+    ready(("qkv_mat", 0), ("qkv_mat", 1), ("qkv_mat", 2), "doc", "qry")
+
+    def first_norm(index):
+        rows = aligned(128 * index, 128, 128)
+        part = dot(mixed[rows, 0:D], down[0:D], 1, 1)
+        part = part + dot(mixed[rows, D : 2 * D], down[D : 2 * D], 1, 1)
+        part = part + dot(mixed[rows, 2 * D : 3 * D], down[2 * D : 3 * D], 1, 1)
+        here = aligned(3 * D + 128 * index, 128, 128)
+        grad, terms = norm_back(down[here].astype(F32), gains[0:1, :], part)
+        down[here] = (residual[rows] + grad).astype(BF)
+        gain_terms[0] = gain_terms[0] + terms
+
+    lax.fori_loop(0, 3, lambda index, carry: (first_norm(index), carry)[1], 0)
+    scatter.step(turn)
+    turn = turn + 1
+    lax.fori_loop(3, 6, lambda index, carry: (first_norm(index), carry)[1], 0)
+    stores = [
+        pltpu.make_async_copy(down.at[pl.ds(3 * D, 512)], doc_grad, load_sem.at[len(loads)]),
+        pltpu.make_async_copy(
+            down.at[pl.ds(3 * D + 512, 256)], qry_grad, load_sem.at[len(loads) + 1]
+        ),
+    ]
+    for copy in stores:
+        copy.start()
+
+    small[0] = jnp.zeros((40, 128), F32)
+    for row in range(3):
+        total = jnp.sum(gain_terms[row], axis=0, keepdims=True)
+        for tile in range(6):
+            line = 6 * row + tile
+            small[0, line : line + 1, :] = total[:, 128 * tile : 128 * tile + 128]
+    column = lax.broadcasted_iota(jnp.int32, (BUCKETS, 512), 1)
+    relative = jnp.where(column < 384, column - 128, column - 640)
+    marks = marks_of(relative).astype(F32)
+    small[0, 24:40, 0:BUCKETS] = lax.dot_general(
+        diagonal_rows[...],
+        marks,
+        (((1,), (1,)), ((), ())),
+        precision=lax.Precision.HIGHEST,
+        preferred_element_type=F32,
+    )
+
+    def small_copy(index):
+        device = ([place.to_sib, place.to_x, place.to_y] + place.to_z)[index]
+        return remote(
+            small.at[min(index, 3)],
+            small_in.at[index],
+            small_send.at[index],
+            small_recv.at[index],
+            device,
+        )
+
+    small_copy(0).start()
+    for index in range(3):
+        scatter.step(turn)
+        turn = turn + 1
+        small_copy(index).wait_recv()
+        small[index + 1] = small[index] + small_in[index]
+        if index < 2:
+            small_copy(index + 1).start()
+    for k in range(3):
+        small_copy(3 + k).start()
+    scatter.step(turn)
+    for k in range(3):
+        small_copy(3 + k).wait_recv()
+    total = jnp.zeros((40, 128), F32)
+    for other in range(4):
+        piece = small[3]
+        for k in range(3):
+            here = lax.rem(place.z + 3 - k, 4) == other
+            piece = jnp.where(here, small_in[3 + k], piece)
+        total = total + piece
+    small_out[...] = total
+
+    scatter.finish()
+    for index in range(6):
+        small_copy(index).wait_send()
+    for copy in stores:
+        copy.wait()
+
+
+def backward(doc, qry, doc_cotangent, qry_cotangent, gains, saved):
+    vmem = pl.BlockSpec(memory_space=pltpu.VMEM)
+    hbm = pl.BlockSpec(memory_space=pl.ANY)
+    dma = pltpu.SemaphoreType.DMA
+    scratch = [
+        pltpu.VMEM((768, D + PROJ), BF),
+        pltpu.VMEM((FF, D), BF),
+        pltpu.VMEM((2, 768, 1536), BF),
+        pltpu.VMEM((2, 768, 1536), BF),
+        pltpu.VMEM((768, FF), BF),
+        pltpu.VMEM((768, D), F32),
+        pltpu.VMEM((768, D), F32),
+        pltpu.VMEM((768, D), F32),
+        pltpu.VMEM((768, D), BF),
+        pltpu.VMEM((768, D), BF),
+        pltpu.VMEM((768, D), BF),
+        pltpu.VMEM((768, D), BF),
+        pltpu.VMEM((768, PROJ), BF),
+        pltpu.VMEM((3, 8, D), F32),
+        pltpu.VMEM((16, 512), F32),
+        pltpu.VMEM((512, 512), F32),
+        pltpu.VMEM((4, 40, 128), F32),
+        pltpu.VMEM((6, 40, 128), F32),
+    ]
+    scratch += Scatter.scratch() + Scatter.semaphores() + [dma((6,)), dma((6,)), dma((36,))]
+    lines = (144, 144, 144, 144, 576, 576, 576, 24)
+    return pl.pallas_call(
+        backward_kernel,
+        out_shape=(
+            jax.ShapeDtypeStruct((512, D), BF),
+            jax.ShapeDtypeStruct((256, D), BF),
+        )
+        + tuple(jax.ShapeDtypeStruct((count, 128), F32) for count in lines)
+        + (jax.ShapeDtypeStruct((40, 128), F32),),
+        in_specs=[hbm, hbm, vmem, vmem, vmem] + [hbm] * len(saved),
+        out_specs=(hbm, hbm) + (vmem,) * 9,
+        scratch_shapes=scratch,
+        compiler_params=pltpu.CompilerParams(
+            collective_id=1, has_side_effects=True, vmem_limit_bytes=VMEM_LIMIT
+        ),
+        name="backward",
+    )(doc, qry, doc_cotangent, qry_cotangent, gains, *saved)
+
+
+def local_fast(
+    document_tokens,
+    document_lengths,
+    query_tokens,
+    query_lengths,
+    weight_query,
+    weight_key,
+    weight_value,
+    weight_out,
+    weight_gate,
+    weight_up,
+    weight_down,
+    weight_proj,
+    norm_gains,
+    rel_table,
+    document_cotangent,
+    query_cotangent,
+):
+    doc = document_tokens.reshape(DOC_LEN, D)
+    qry = query_tokens.reshape(-1, D)
+    units = norm_gains.astype(jnp.float32).reshape(9, 64)
+    units = jnp.pad(jnp.concatenate([units, units], axis=1), ((0, 7), (0, 0)))
+    table = jnp.pad(rel_table.astype(jnp.float32).reshape(8, HEADS), ((0, 0), (0, 128 - HEADS)))
+    small = jnp.concatenate([units, table], axis=0)
+    flats = [
+        w.reshape(-1, 128)
+        for w in (
+            weight_query,
+            weight_key,
+            weight_value,
+            weight_out,
+            weight_gate,
+            weight_up,
+            weight_down,
+            weight_proj,
+        )
+    ]
+    results = forward(doc, qry, document_lengths, query_lengths.reshape(1, 8), small, flats)
+    doc_out, qry_out, gains = results[0:3]
+    grads = backward(
+        doc,
+        qry,
+        document_cotangent.reshape(DOC_LEN, PROJ),
+        query_cotangent.reshape(-1, PROJ),
+        gains,
+        results[3:],
+    )
+    fsdp_index = lax.axis_index("fsdp")
+    small = grads[10]
+    own_gains = lax.dynamic_slice_in_dim(small[0:18].reshape(-1), fsdp_index * 576, 576)
+    own_table = lax.dynamic_slice_in_dim(small[24 : 24 + HEADS], fsdp_index * 8, 8, 1)
+    return (
+        doc_out.reshape(document_cotangent.shape),
+        qry_out.reshape(query_cotangent.shape),
+        grads[0].reshape(document_tokens.shape),
+        grads[1].reshape(query_tokens.shape),
+        *[grad.reshape(-1) for grad in grads[2:10]],
+        own_gains,
+        jnp.transpose(own_table).reshape(-1),
+    )
+
+
 def solution(mesh):
     placed = (
         P(("dp", "fsdp"), None, None),
@@ -375,7 +1664,7 @@
         P(("dp", "fsdp"), None, None),
     )
     return jax.shard_map(
-        local,
+        local_fast if (mesh.shape["dp"], mesh.shape["fsdp"]) == (8, 4) else local,
         mesh=mesh,
         in_specs=placed,
         out_specs=(

time: 1250 us -> 264 us (0.21)
  waiting for transfers between devices: 647 us -> 0 us
  local copies, waits for them, and re-layouts: 278 us -> 18.4 us
  Pallas kernels: 0 us -> 241 us
  matrix products: 156 us -> 0 us
  blocking collectives: 126 us -> 0 us
  other arithmetic: 16.7 us -> 0.69 us
  between operations: 16.8 us -> 0.91 us
    unnamed x9 -> x0, waiting for transfers between devices: 470 us -> none
    pallas_call x0 -> x2, Pallas kernels: none -> 241 us  [the longest x1 123 us: forward(): pl.pallas_call(forward_kernel, out_shape=(jax.ShapeDtypeStruct((512, PROJ...]
    all_gather x7 -> x0, waiting for transfers between devices: 177 us -> none  [the longest x1 56.8 us: local(): lax.all_gather(weight_up, ('dp', 'fsdp'), axis=0, tiled=True)]
    dot_general x40 -> x0, matrix products: 156 us -> none  [the longest x8 37.9 us: times_transposed(): lax.dot_general(left_rows, matrix, (((1,), (1,)), ((), ())), preferred_el...]
    reshape x38 -> x4, local copies, waits for them, and re-layouts: 134 us -> 2.89 us  [the longest x1 0.78 us: local_fast(): small[0:18].reshape(-1)]
    unnamed x217 -> x24, local copies, waits for them, and re-layouts: 119 us -> 14 us
    all_gather x1 -> x0, blocking collectives: 70.2 us -> none  [local(): lax.all_gather(weight_proj, ('dp', 'fsdp'), axis=0, tiled=True)]
    psum x1 -> x0, blocking collectives: 41.9 us -> none  [local(): gain_whole, table_whole = lax.psum((gain_grads, table_flat), ('dp', 'fsdp'))]
  transfers between devices with their start and end apart: 8 -> 0, of which waited for: 6 -> 0; matrix products, arithmetic and copies ran while one was open for 16% -> 0% of each run, Pallas kernels for 0% -> 0%
where the time goes in v2:
time: 264 us; the launch traced here: 261 us
  Pallas kernels  241 us (91%)
  local copies, waits for them, and re-layouts  18.4 us (7%)
    pallas_call x1, Pallas kernels, forward(): pl.pallas_call(forward_kernel, out_shape=(jax.ShapeDtypeStruct((512, PROJ...  123 us
    pallas_call x1, Pallas kernels, backward(): pl.pallas_call(backward_kernel, out_shape=(jax.ShapeDtypeStruct((512, D),...  118 us
    unnamed x24, local copies, waits for them, and re-layouts  14 us

profile of v2, /device:TPU:0, one launch (start us, length us, event | category | flops | bytes accessed | tf_op | source)
XLA Modules:
  0.0 261.2 jit_solution(17676687280723018379)
XLA Ops:
  0.6 0.7 reshape.121
  1.4 0.8 reshape.120
  2.2 0.1 fusion.5
  2.2 0.6 fusion.4.refs_4_
  2.8 123.4 %forward.1 = (bf16[512,128]{1,0:T(8,128)(2,1)}, bf16[256,128]{1,0:T(8,128)(2,1)}, f32[8,768]{1,0:T(8,128)}, bf16[768,2304]{1,0:T(8,128)(2,1)}, bf16[768,896]{1,0...) custom-call(bf16[512,768]{1,0:T(8,128)(2,1)} %bitcast.29, ...), custom_call_target="tpu_custom_call" | custom-call | tf_op jit(solution)/shard_map/forward/pallas_call | solution.py:1131
  126.3 0.0 copy-start.3
  126.3 0.0 copy-start.4
  126.3 117.7 %backward.1 = (bf16[512,768]{1,0:T(8,128)(2,1)}, bf16[256,768]{1,0:T(8,128)(2,1)}, f32[144,128]{1,0:T(8,128)}, f32[144,128]{1,0:T(8,128)}, f32[144,128]{1,0:T(8,...) custom-call(bf16[512,768]{1,0:T(8,128)(2,1)} %bitcast.30, ...), custom_call_target="tpu_custom_call" | custom-call | tf_op jit(solution)/shard_map/backward/pallas_call | solution.py:1567
  244.0 0.0 copy-start.2
  244.0 0.0 copy-start.1
  244.1 0.0 copy-start
  244.1 0.0 copy-start.5
  244.1 0.8 slice_bitcast_fusion
  244.9 0.7 dynamic_slice.6
  245.5 0.7 slice.7
  246.2 0.1 dynamic-slice_bitcast_fusion
  246.3 0.1 copy.30
  246.4 0.6 reshape.145
  247.0 0.0 copy-done.3
  247.0 0.7 copy.43
  247.6 0.0 copy-done.4
  247.6 0.6 copy.44
  248.3 2.1 copy.45
  250.3 1.8 copy.46
  252.1 1.5 copy.47
  253.6 1.5 copy.48
  255.2 1.5 copy.49
  256.7 1.5 copy.50
  258.2 0.0 copy-done.2
  258.2 0.7 copy.51
  258.9 0.0 copy-done.1
  258.9 0.7 copy.52
  259.7 0.0 copy-done
  259.7 0.7 copy.53
  260.4 0.0 copy-done.5
  260.4 0.6 copy.54
Async XLA Ops:
  126.3 120.7 %copy-start.3 = (bf16[512,128]{1,0:T(8,128)(2,1)S(1)}, bf16[512,128]{1,0:T(8,128)(2,1)}, u32[]{:S(2)}) copy-start(bf16[512,128]{1,0:T(8,128)(2,1)} %get-tuple-element.43) | copy-start | bytes 393220
  126.3 121.4 %copy-start.4 = (bf16[256,128]{1,0:T(8,128)(2,1)S(1)}, bf16[256,128]{1,0:T(8,128)(2,1)}, u32[]{:S(2)}) copy-start(bf16[256,128]{1,0:T(8,128)(2,1)} %get-tuple-element.44) | copy-start | bytes 196612
  244.0 14.2 %copy-start.2 = (f32[576,128]{1,0:T(8,128)S(1)}, f32[576,128]{1,0:T(8,128)}, u32[]{:S(2)}) copy-start(f32[576,128]{1,0:T(8,128)} %get-tuple-element.67) | copy-start | bytes 884740
  244.0 14.9 %copy-start.1 = (f32[576,128]{1,0:T(8,128)S(1)}, f32[576,128]{1,0:T(8,128)}, u32[]{:S(2)}) copy-start(f32[576,128]{1,0:T(8,128)} %get-tuple-element.68) | copy-start | bytes 884740
  244.1 15.6 %copy-start = (f32[576,128]{1,0:T(8,128)S(1)}, f32[576,128]{1,0:T(8,128)}, u32[]{:S(2)}) copy-start(f32[576,128]{1,0:T(8,128)} %get-tuple-element.69) | copy-start | bytes 884740
  244.1 16.3 %copy-start.5 = (f32[24,128]{1,0:T(8,128)S(1)}, f32[24,128]{1,0:T(8,128)}, u32[]{:S(2)}) copy-start(f32[24,128]{1,0:T(8,128)} %get-tuple-element.70) | copy-start | bytes 36868
